TPU v7x, 128 devices: a whole 4x4x4 slice. The times are simulated.
128 devices in a mesh: slab: 8 (over x_lo, y), grp: 16 (over x_hi, z, core).
Axes of the slice: x: 4 (x_hi: 2, x_lo: 2; x = x_hi * 2 + x_lo), y: 4, z: 4, core: 2. Of those that a mesh axis runs over, the one named last changes fastest.
Arguments:
- cell_density: float32 [8, 32, 2, 8], P('slab', 'grp'), may hold values from 1 to 10
- cell_slot: int32 [8, 32, 2, 8], P('slab', 'grp'), may hold values from 0 to 7, each once within a row
- neighbours: int32 [8, 32, 2, 6], P('slab', 'grp'), may hold values from -1 to 511, as said below
- face_code: int32 [8, 32, 2, 6], P('slab', 'grp'), may hold values from 0 to 15, as said below
- stiffness: float32 [64, 64], replicated, as said below
- prolong: float32 [8, 64, 64], replicated, as said below
- penalty: float32 [16, 64, 64], replicated, as said below
- fine_rhs: bfloat16 [8, 32, 2, 8, 4096], P('slab', 'grp'), may hold values from -24 to 24
Outputs:
- coarse_correction: float32 [8, 32, 2, 4096], P(None, 'grp')
Inputs may be any that keep to these rules, and one draw needn't show every extreme that they name: `neighbours`: aggregates form a lattice of 8 x 32 x 2; faces in the order -first, +first, -second, +second, -third, +third dimension. Each entry is the number of the lattice neighbour across that face, or -1 where the face lies on the lattice boundary or is a wall; a wall seen from one side is a wall from the other. `face_code`: equal on both sides of every face that is not -1 in neighbours. `cell_slot`: the 8 cells of each aggregate hold each slot once. `stiffness`: Symmetric, each diagonal entry larger than the sum of the magnitudes of the other entries of its row. `prolong`: each diagonal entry larger than the sum of the magnitudes of the other entries of its row. `penalty`: Symmetric, each diagonal entry larger than the sum of the magnitudes of the other entries of its row.
All inputs are finite; a program needn't handle non-finite values.
Results may differ from a plain program's by a relative error of at most 0.0003.
Values sent between devices are 32-bit elements; how exact they have to be, the bound alone decides.
A program may use at most 128 MiB of HBM per device.

v0:
```python
import jax
import jax.numpy as jnp
from jax import lax
from jax.sharding import PartitionSpec as P

SWEEPS = 8


highest = lax.Precision.HIGHEST


def extended(block, sides, width):
    for axis, dim in sides:
        count = lax.axis_size(axis)
        forward = [(i, i + 1) for i in range(count - 1)]
        backward = [(target, source) for source, target in forward]
        low = lax.ppermute(
            lax.slice_in_dim(block, block.shape[dim] - width, None, axis=dim), axis, forward
        )
        high = lax.ppermute(lax.slice_in_dim(block, 0, width, axis=dim), axis, backward)
        block = jnp.concatenate([low, block, high], axis=dim)
    return block


def assemble(weights, code_hot, templates, penalty):
    kids = templates.shape[0]
    dof_count = templates.shape[1]
    code_count = penalty.shape[0]
    leading = weights.shape[:-1]
    flat_templ = templates.reshape(kids, dof_count * dof_count)
    flat_pen = penalty.reshape(code_count, dof_count * dof_count)
    cell_part = jnp.dot(weights.reshape(-1, kids), flat_templ, precision=highest)
    face_part = jnp.dot(
        jnp.sum(code_hot, axis=-2).reshape(-1, code_count), flat_pen, precision=highest
    )
    diag_flat = (cell_part + face_part).reshape(leading + (dof_count * dof_count,))
    off_flat = (-jnp.dot(code_hot.reshape(-1, code_count), flat_pen, precision=highest)).reshape(
        leading + (6, dof_count * dof_count)
    )
    return (diag_flat, off_flat)


def as_blocks(flat_blocks, dof_count):
    return flat_blocks.reshape(flat_blocks.shape[:-1] + (dof_count, dof_count))


def largest_ratio(diag_flat, off_flat, dof_count):
    diag_blocks = as_blocks(diag_flat, dof_count)
    off_blocks = as_blocks(off_flat, dof_count)
    jacobi = jnp.diagonal(diag_blocks, axis1=-2, axis2=-1)
    totals = jnp.sum(jnp.abs(diag_blocks), axis=-1) + jnp.sum(jnp.abs(off_blocks), axis=(-3, -1))
    return jnp.max(totals / jacobi)


def block_apply(blocks, vector):
    return jnp.einsum("abcij,abcjr->abcir", blocks, vector, precision=highest)


def faces_sum(vector, spread, diag_blocks, off_blocks):
    views = [
        spread[:-2, 1:-1, 1:-1],
        spread[2:, 1:-1, 1:-1],
        spread[1:-1, :-2, 1:-1],
        spread[1:-1, 2:, 1:-1],
        spread[1:-1, 1:-1, :-2],
        spread[1:-1, 1:-1, 2:],
    ]
    result = block_apply(diag_blocks, vector)
    for face in range(6):
        result = result + block_apply(off_blocks[:, :, :, face], views[face].reshape(vector.shape))
    return result


def apply_column(vector, diag_blocks, off_blocks):
    rows_a, rows_b, rows_c, dof_count, rhs_count = vector.shape
    flat = vector.reshape(rows_a, rows_b, rows_c, dof_count * rhs_count)
    framed = extended(flat, (("grp", 1),), 1)
    spread = jnp.pad(framed, ((1, 1), (0, 0), (1, 1), (0, 0)))
    return faces_sum(vector, spread, diag_blocks, off_blocks)


def chebyshev(resid, diag_blocks, off_blocks, upper, operator):
    jacobi = jnp.diagonal(diag_blocks, axis1=-2, axis2=-1)[..., None]
    lower = upper / 10.0
    centre_val = 0.5 * (upper + lower)
    half_width = 0.5 * (upper - lower)
    sigma_val = centre_val / half_width
    damping = 1.0 / sigma_val
    update = resid / jacobi / centre_val
    solution = update
    for sweep in range(SWEEPS):
        resid = resid - operator(update, diag_blocks, off_blocks)
        damping_next = 1.0 / (2.0 * sigma_val - damping)
        update = damping_next * damping * update + 2.0 * damping_next / half_width * (
            resid / jacobi
        )
        solution = solution + update
        damping = damping_next
    return solution


def local(cell_density, cell_slot, neighbours, face_code, stiffness, prolong, penalty, fine_rhs):
    rows_a, rows_b, rows_c, kids = cell_density.shape
    dof_count = stiffness.shape[0]
    code_count = penalty.shape[0]
    rhs_count = fine_rhs.shape[-1] // dof_count
    templates = jnp.einsum("sji,jk,skl->sil", prolong, stiffness, prolong, precision=highest)
    mean_rho = jnp.mean(cell_density, axis=3)
    framed = extended(mean_rho, (("slab", 0), ("grp", 1)), 1)
    centre = framed[1:-1, 1:-1]
    spaced = jnp.pad(centre, ((0, 0), (0, 0), (1, 1)))
    others = jnp.stack(
        [
            framed[:-2, 1:-1],
            framed[2:, 1:-1],
            framed[1:-1, :-2],
            framed[1:-1, 2:],
            spaced[:, :, :-2],
            spaced[:, :, 2:],
        ],
        axis=-1,
    )
    present = neighbours >= 0
    face_weight = jnp.where(present, 2.0 / (centre[..., None] + others), jnp.float32(0.0))
    code_hot = (face_code[..., None] == jnp.arange(code_count, dtype=jnp.int32)).astype(
        jnp.float32
    ) * face_weight[..., None]
    onehot = (cell_slot[..., None] == jnp.arange(kids, dtype=jnp.int32)).astype(jnp.float32)
    weights = jnp.einsum("abcq,abcqs->abcs", 1.0 / cell_density, onehot, precision=highest)
    cell_prolong = jnp.einsum("abcqs,sji->abcqji", onehot, prolong, precision=highest)
    cell_rhs = fine_rhs.reshape(rows_a, rows_b, rows_c, kids, dof_count, rhs_count).astype(
        jnp.float32
    )
    coarse_rhs = jnp.einsum("abcqji,abcqjr->abcir", cell_prolong, cell_rhs, precision=highest)
    coarse_rhs = coarse_rhs.reshape(rows_a, rows_b, rows_c, dof_count * rhs_count)
    own_diag, own_off = assemble(weights, code_hot, templates, penalty)
    diag_all, off_all, rhs_all = (
        lax.all_gather(own_diag, "slab", axis=0, tiled=True),
        lax.all_gather(own_off, "slab", axis=0, tiled=True),
        lax.all_gather(coarse_rhs, "slab", axis=0, tiled=True),
    )
    upper = lax.pmax(largest_ratio(diag_all, off_all, dof_count), "grp")
    resid = rhs_all.reshape(rhs_all.shape[:-1] + (dof_count, rhs_count))
    solution = chebyshev(
        resid, as_blocks(diag_all, dof_count), as_blocks(off_all, dof_count), upper, apply_column
    )
    return solution.reshape(solution.shape[:3] + (dof_count * rhs_count,))


def solution(mesh):
    return jax.shard_map(
        local,
        mesh=mesh,
        in_specs=(
            P("slab", "grp", None, None),
            P("slab", "grp", None, None),
            P("slab", "grp", None, None),
            P("slab", "grp", None, None),
            P(),
            P(),
            P(),
            P("slab", "grp", None, None, None),
        ),
        out_specs=P(None, "grp", None, None),
        check_vma=False,
    )
```

profile of v0, /device:TPU:121, one launch (start us, length us, event | category | flops | bytes accessed | tf_op | source)
XLA Modules:
  0.0 649.8 jit_solution(2406266245142685637)
XLA Ops:
  16.7 5.0 collective-permute-start.2
  23.8 6.4 collective-permute-done.3
  36.9 26.6 %all_gather.9 = f32[8,2,2,4096]{3,2,1,0:T(2,128)S(1)} all-gather(f32[1,2,2,4096]{3,2,1,0:T(2,128)S(1)} %reshape.377), channel_id=1, replica_groups=mesh['slab'=8,'grp'=16] {'slab'}, dimensions={0}, use_global_device_ids=true | all-gather | bytes 589824 | tf_op jit(solution)/shard_map/all_gather | solution.py:140
  65.1 25.1 %all_gather.10 = f32[8,2,2,4096]{3,2,1,0:T(2,128)S(1)} all-gather(f32[1,2,2,4096]{3,2,1,0:T(2,128)S(1)} %reshape.384), channel_id=1, replica_groups=mesh['slab'=8,'grp'=16] {'slab'}, dimensions={0}, use_global_device_ids=true | all-gather | bytes 589824 | tf_op jit(solution)/shard_map/all_gather | solution.py:138
  90.8 8.6 %copy.69 = f32[8,2,2,64,64]{0,2,4,3,1:T(2,128)} copy(f32[8,2,2,64,64]{4,3,2,1,0:T(8,128)S(1)} %reshape.385) | data formatting | bytes 1048576 | tf_op jit(solution)/shard_map/reshape | solution.py:44
  112.3 36.2 %pmax.7 = f32[]{:T(128)} all-reduce(f32[]{:T(128)} %fusion.87), channel_id=1, replica_groups=mesh['slab'=8,'grp'=16] {'grp'}, use_global_device_ids=true, to_apply=%region_6.7 | all-reduce | flops 1 | bytes 8 | tf_op jit(solution)/shard_map/pmax | solution.py:142
  156.8 7.8 %collective-permute-start.4 = (f32[8,1,2,4096]{3,2,1,0:T(2,128)}, f32[8,1,2,4096]{3,2,1,0:T(2,128)S(1)}, u32[]{:S(2)}, u32[]{:S(2)}) collective-permute-start(f32[8,1,2,4096]{3,2,1,0:T(2,128)} %get-tuple-element.67), channel_id=1, source_target_pairs={{0,1},{1,2},{2,3},{3,4},{4,5},{5,6},{6,7},{7,8},{8,9},{9,10},{10,1... | collective-permute-start | bytes 786440 | tf_op jit(solution)/shard_map/ppermute | solution.py:17
  170.5 6.9 %reshape.387 = f32[8,2,2,6,64,64]{5,4,2,1,0,3:T(8,128)} reshape(f32[8,2,2,6,4096]{4,2,1,0,3:T(2,128)} %copy.75) | data formatting | bytes 6291456 | tf_op jit(solution)/shard_map/reshape | solution.py:44
  215.2 5.0 multiply_add_fusion.6
  220.7 7.3 %collective-permute-start.6 = (f32[8,1,2,4096]{3,2,1,0:T(2,128)S(1)}, f32[8,1,2,4096]{3,2,1,0:T(2,128)S(1)}, u32[]{:S(2)}, u32[]{:S(2)}) collective-permute-start(f32[8,1,2,4096]{3,2,1,0:T(2,128)S(1)} %get-tuple-element.63), channel_id=1, source_target_pairs={{0,1},{1,2},{2,3},{3,4},{4,5},{5,6},{6,7},{7,8},{8,9},{9,10},{10,1... | collective-permute-start | bytes 786440 | tf_op jit(solution)/shard_map/ppermute | solution.py:17
  232.1 7.2 %collective-permute-done.7 = f32[8,1,2,4096]{3,2,1,0:T(2,128)S(1)} collective-permute-done((f32[8,1,2,4096]{3,2,1,0:T(2,128)S(1)}, f32[8,1,2,4096]{3,2,1,0:T(2,128)S(1)}, u32[]{:S(2)}, u32[]{:S(2)}) %collective-permute-start.7) | collective-permute-done | bytes 262176 | tf_op jit(solution)/shard_map/ppermute | solution.py:20
  273.3 4.8 multiply_add_fusion.5
  285.2 6.6 %collective-permute-done.9 = f32[8,1,2,4096]{3,2,1,0:T(2,128)S(1)} collective-permute-done((f32[8,1,2,4096]{3,2,1,0:T(2,128)S(1)}, f32[8,1,2,4096]{3,2,1,0:T(2,128)S(1)}, u32[]{:S(2)}, u32[]{:S(2)}) %collective-permute-start.9) | collective-permute-done | bytes 262176 | tf_op jit(solution)/shard_map/ppermute | solution.py:20
  325.9 5.0 multiply_add_fusion.4
  339.9 6.6 %collective-permute-done.11 = f32[8,1,2,4096]{3,2,1,0:T(2,128)S(1)} collective-permute-done((f32[8,1,2,4096]{3,2,1,0:T(2,128)S(1)}, f32[8,1,2,4096]{3,2,1,0:T(2,128)S(1)}, u32[]{:S(2)}, u32[]{:S(2)}) %collective-permute-start.11) | collective-permute-done | bytes 262176 | tf_op jit(solution)/shard_map/ppermute | solution.py:20
  387.3 5.2 multiply_add_fusion.3
  403.9 5.5 collective-permute-done.13
  450.1 5.7 multiply_add_fusion.2
  467.2 5.5 collective-permute-done.15
  513.4 5.5 multiply_add_fusion.1
  530.3 5.5 collective-permute-done.17
  576.4 5.5 multiply_add_fusion
  593.3 5.5 collective-permute-done.19
  633.0 7.0 %fusion.46 = f32[8,2,2,64,64]{4,3,2,1,0:T(8,128)} fusion(f32[8,2,2,64,64]{4,3,2,1,0:T(8,128)} %get-tuple-element.92, f32[8,2,2,64,64]{4,3,2,1,0:T(8,128)} %fusion.72, f32[8,2,2,64,64]{4,3,2,1,0:T(8,128)} %fusion.64, f32[8,2,2,64,64]{4,3,2,1,0:T(8,128)} %fusion.56, f32[8,2,2,64,64]{4,3,2,1,0:T(8,128)} %fusion.48, ...), kind=kOutput, calls=%fused_computation.86 | convolution fusion | flops 103153664 | bytes 13647880 | tf_op jit(solution)/shard_map/abcij,abcjr->abcir/dot_general | solution.py:56
  (328 shorter events, 416.6 us)
Async XLA Ops:
  6.5 97.5 %all-gather.2.cloned.1.call-start = ((), (), s32[]{:S(2)}) async-start(), calls=%async_computation | async-start | bytes 3538944 | tf_op jit(solution)/shard_map/all_gather | solution.py:139
  7.4 27.2 %copy-start.51 = (bf16[1,2,2,8,4096]{4,3,2,1,0:T(8,128)(2,1)S(1)}, bf16[1,2,2,8,4096]{4,3,2,1,0:T(8,128)(2,1)}, u32[]{:S(2)}) copy-start(bf16[1,2,2,8,4096]{4,3,2,1,0:T(8,128)(2,1)} %param.15) | copy-start | bytes 786436
  7.4 7.4 %collective-permute-start = (f32[1,2,2]{2,1,0:T(2,128)S(1)}, f32[1,2,2]{2,1,0:T(2,128)S(1)}, u32[]{:S(2)}, u32[]{:S(2)}) collective-permute-start(f32[1,2,2]{2,1,0:T(2,128)S(1)} %get-tuple-element.76), channel_id=1, source_target_pairs={{0,16},{16,32},{32,48},{48,64},{64,80},{80,96},{96,112},{1,17},{17... | collective-permute-start | bytes 56 | tf_op jit(solution)/shard_map/ppermute | solution.py:17
  10.3 6.4 collective-permute-start.1
  16.7 7.1 %collective-permute-start.2 = (f32[3,1,2]{2,1,0:T(1,128)S(1)}, f32[3,1,2]{2,1,0:T(1,128)S(1)}, u32[]{:S(2)}, u32[]{:S(2)}) collective-permute-start(f32[3,1,2]{2,1,0:T(1,128)S(1)} %get-tuple-element.72), channel_id=1, source_target_pairs={{0,1},{1,2},{2,3},{3,4},{4,5},{5,6},{6,7},{7,8},{8,9},{9,10},{10,1... | collective-permute-start | bytes 80 | tf_op jit(solution)/shard_map/ppermute | solution.py:17
  21.7 8.5 %collective-permute-start.3 = (f32[3,1,2]{2,1,0:T(1,128)S(1)}, f32[3,1,2]{2,1,0:T(1,128)S(1)}, u32[]{:S(2)}, u32[]{:S(2)}) collective-permute-start(f32[3,1,2]{2,1,0:T(1,128)S(1)} %get-tuple-element.71), channel_id=1, source_target_pairs={{1,0},{2,1},{3,2},{4,3},{5,4},{6,5},{7,6},{8,7},{9,8},{10,9},{11,1... | collective-permute-start | bytes 80 | tf_op jit(solution)/shard_map/ppermute | solution.py:20
  64.1 151.1 %copy-start.10 = (f32[8,2,2,64,64]{4,3,2,1,0:T(8,128)}, f32[8,2,2,64,64]{4,3,2,1,0:T(8,128)S(1)}, u32[]{:S(2)}) copy-start(f32[8,2,2,64,64]{4,3,2,1,0:T(8,128)S(1)} %reshape.378) | copy-start | bytes 1572868
  156.8 23.2 %collective-permute-start.4 = (f32[8,1,2,4096]{3,2,1,0:T(2,128)}, f32[8,1,2,4096]{3,2,1,0:T(2,128)S(1)}, u32[]{:S(2)}, u32[]{:S(2)}) collective-permute-start(f32[8,1,2,4096]{3,2,1,0:T(2,128)} %get-tuple-element.67), channel_id=1, source_target_pairs={{0,1},{1,2},{2,3},{3,4},{4,5},{5,6},{6,7},{7,8},{8,9},{9,10},{10,1... | collective-permute-start | bytes 786440 | tf_op jit(solution)/shard_map/ppermute | solution.py:17
  164.6 15.4 %collective-permute-start.5 = (f32[8,1,2,4096]{3,2,1,0:T(2,128)S(1)}, f32[8,1,2,4096]{3,2,1,0:T(2,128)S(1)}, u32[]{:S(2)}, u32[]{:S(2)}) collective-permute-start(f32[8,1,2,4096]{3,2,1,0:T(2,128)S(1)} %get-tuple-element.68), channel_id=1, source_target_pairs={{1,0},{2,1},{3,2},{4,3},{5,4},{6,5},{7,6},{8,7},{9,8},{10,9},{11,1... | collective-permute-start | bytes 786440 | tf_op jit(solution)/shard_map/ppermute | solution.py:20
  220.2 53.1 %copy-start.8 = (f32[8,2,2,64,64]{4,3,2,1,0:T(8,128)}, f32[8,2,2,64,64]{4,3,2,1,0:T(8,128)S(1)}, u32[]{:S(2)}) copy-start(f32[8,2,2,64,64]{4,3,2,1,0:T(8,128)S(1)} %get-tuple-element.79) | copy-start | bytes 1572868
  220.7 11.4 %collective-permute-start.6 = (f32[8,1,2,4096]{3,2,1,0:T(2,128)S(1)}, f32[8,1,2,4096]{3,2,1,0:T(2,128)S(1)}, u32[]{:S(2)}, u32[]{:S(2)}) collective-permute-start(f32[8,1,2,4096]{3,2,1,0:T(2,128)S(1)} %get-tuple-element.63), channel_id=1, source_target_pairs={{0,1},{1,2},{2,3},{3,4},{4,5},{5,6},{6,7},{7,8},{8,9},{9,10},{10,1... | collective-permute-start | bytes 786440 | tf_op jit(solution)/shard_map/ppermute | solution.py:17
  228.0 11.3 %collective-permute-start.7 = (f32[8,1,2,4096]{3,2,1,0:T(2,128)S(1)}, f32[8,1,2,4096]{3,2,1,0:T(2,128)S(1)}, u32[]{:S(2)}, u32[]{:S(2)}) collective-permute-start(f32[8,1,2,4096]{3,2,1,0:T(2,128)S(1)} %get-tuple-element.64), channel_id=1, source_target_pairs={{1,0},{2,1},{3,2},{4,3},{5,4},{6,5},{7,6},{8,7},{9,8},{10,9},{11,1... | collective-permute-start | bytes 786440 | tf_op jit(solution)/shard_map/ppermute | solution.py:20
  278.7 6.6 %collective-permute-start.8 = (f32[8,1,2,4096]{3,2,1,0:T(2,128)S(1)}, f32[8,1,2,4096]{3,2,1,0:T(2,128)S(1)}, u32[]{:S(2)}, u32[]{:S(2)}) collective-permute-start(f32[8,1,2,4096]{3,2,1,0:T(2,128)S(1)} %get-tuple-element.59), channel_id=1, source_target_pairs={{0,1},{1,2},{2,3},{3,4},{4,5},{5,6},{6,7},{7,8},{8,9},{9,10},{10,1... | collective-permute-start | bytes 786440 | tf_op jit(solution)/shard_map/ppermute | solution.py:17
  280.6 11.3 %collective-permute-start.9 = (f32[8,1,2,4096]{3,2,1,0:T(2,128)S(1)}, f32[8,1,2,4096]{3,2,1,0:T(2,128)S(1)}, u32[]{:S(2)}, u32[]{:S(2)}) collective-permute-start(f32[8,1,2,4096]{3,2,1,0:T(2,128)S(1)} %get-tuple-element.60), channel_id=1, source_target_pairs={{1,0},{2,1},{3,2},{4,3},{5,4},{6,5},{7,6},{8,7},{9,8},{10,9},{11,1... | collective-permute-start | bytes 786440 | tf_op jit(solution)/shard_map/ppermute | solution.py:20
  333.3 6.6 %collective-permute-start.10 = (f32[8,1,2,4096]{3,2,1,0:T(2,128)S(1)}, f32[8,1,2,4096]{3,2,1,0:T(2,128)S(1)}, u32[]{:S(2)}, u32[]{:S(2)}) collective-permute-start(f32[8,1,2,4096]{3,2,1,0:T(2,128)S(1)} %get-tuple-element.55), channel_id=1, source_target_pairs={{0,1},{1,2},{2,3},{3,4},{4,5},{5,6},{6,7},{7,8},{8,9},{9,10},{10,1... | collective-permute-start | bytes 786440 | tf_op jit(solution)/shard_map/ppermute | solution.py:17
  335.2 11.3 %collective-permute-start.11 = (f32[8,1,2,4096]{3,2,1,0:T(2,128)S(1)}, f32[8,1,2,4096]{3,2,1,0:T(2,128)S(1)}, u32[]{:S(2)}, u32[]{:S(2)}) collective-permute-start(f32[8,1,2,4096]{3,2,1,0:T(2,128)S(1)} %get-tuple-element.56), channel_id=1, source_target_pairs={{1,0},{2,1},{3,2},{4,3},{5,4},{6,5},{7,6},{8,7},{9,8},{10,9},{11,1... | collective-permute-start | bytes 786440 | tf_op jit(solution)/shard_map/ppermute | solution.py:20
  396.2 7.7 %collective-permute-start.12 = (f32[8,1,2,4096]{3,2,1,0:T(2,128)S(1)}, f32[8,1,2,4096]{3,2,1,0:T(2,128)S(1)}, u32[]{:S(2)}, u32[]{:S(2)}) collective-permute-start(f32[8,1,2,4096]{3,2,1,0:T(2,128)S(1)} %get-tuple-element.51), channel_id=1, source_target_pairs={{0,1},{1,2},{2,3},{3,4},{4,5},{5,6},{6,7},{7,8},{8,9},{9,10},{10,1... | collective-permute-start | bytes 786440 | tf_op jit(solution)/shard_map/ppermute | solution.py:17
  398.1 11.3 %collective-permute-start.13 = (f32[8,1,2,4096]{3,2,1,0:T(2,128)S(1)}, f32[8,1,2,4096]{3,2,1,0:T(2,128)S(1)}, u32[]{:S(2)}, u32[]{:S(2)}) collective-permute-start(f32[8,1,2,4096]{3,2,1,0:T(2,128)S(1)} %get-tuple-element.52), channel_id=1, source_target_pairs={{1,0},{2,1},{3,2},{4,3},{5,4},{6,5},{7,6},{8,7},{9,8},{10,9},{11,1... | collective-permute-start | bytes 786440 | tf_op jit(solution)/shard_map/ppermute | solution.py:20
  459.5 7.7 %collective-permute-start.14 = (f32[8,1,2,4096]{3,2,1,0:T(2,128)S(1)}, f32[8,1,2,4096]{3,2,1,0:T(2,128)S(1)}, u32[]{:S(2)}, u32[]{:S(2)}) collective-permute-start(f32[8,1,2,4096]{3,2,1,0:T(2,128)S(1)} %get-tuple-element.47), channel_id=1, source_target_pairs={{0,1},{1,2},{2,3},{3,4},{4,5},{5,6},{6,7},{7,8},{8,9},{9,10},{10,1... | collective-permute-start | bytes 786440 | tf_op jit(solution)/shard_map/ppermute | solution.py:17
  461.4 11.3 %collective-permute-start.15 = (f32[8,1,2,4096]{3,2,1,0:T(2,128)S(1)}, f32[8,1,2,4096]{3,2,1,0:T(2,128)S(1)}, u32[]{:S(2)}, u32[]{:S(2)}) collective-permute-start(f32[8,1,2,4096]{3,2,1,0:T(2,128)S(1)} %get-tuple-element.48), channel_id=1, source_target_pairs={{1,0},{2,1},{3,2},{4,3},{5,4},{6,5},{7,6},{8,7},{9,8},{10,9},{11,1... | collective-permute-start | bytes 786440 | tf_op jit(solution)/shard_map/ppermute | solution.py:20
  522.5 7.7 %collective-permute-start.16 = (f32[8,1,2,4096]{3,2,1,0:T(2,128)S(1)}, f32[8,1,2,4096]{3,2,1,0:T(2,128)S(1)}, u32[]{:S(2)}, u32[]{:S(2)}) collective-permute-start(f32[8,1,2,4096]{3,2,1,0:T(2,128)S(1)} %get-tuple-element.43), channel_id=1, source_target_pairs={{0,1},{1,2},{2,3},{3,4},{4,5},{5,6},{6,7},{7,8},{8,9},{9,10},{10,1... | collective-permute-start | bytes 786440 | tf_op jit(solution)/shard_map/ppermute | solution.py:17
  524.5 11.3 %collective-permute-start.17 = (f32[8,1,2,4096]{3,2,1,0:T(2,128)S(1)}, f32[8,1,2,4096]{3,2,1,0:T(2,128)S(1)}, u32[]{:S(2)}, u32[]{:S(2)}) collective-permute-start(f32[8,1,2,4096]{3,2,1,0:T(2,128)S(1)} %get-tuple-element.44), channel_id=1, source_target_pairs={{1,0},{2,1},{3,2},{4,3},{5,4},{6,5},{7,6},{8,7},{9,8},{10,9},{11,1... | collective-permute-start | bytes 786440 | tf_op jit(solution)/shard_map/ppermute | solution.py:20
  585.6 7.7 %collective-permute-start.18 = (f32[8,1,2,4096]{3,2,1,0:T(2,128)S(1)}, f32[8,1,2,4096]{3,2,1,0:T(2,128)S(1)}, u32[]{:S(2)}, u32[]{:S(2)}) collective-permute-start(f32[8,1,2,4096]{3,2,1,0:T(2,128)S(1)} %get-tuple-element.39), channel_id=1, source_target_pairs={{0,1},{1,2},{2,3},{3,4},{4,5},{5,6},{6,7},{7,8},{8,9},{9,10},{10,1... | collective-permute-start | bytes 786440 | tf_op jit(solution)/shard_map/ppermute | solution.py:17
  587.5 11.3 %collective-permute-start.19 = (f32[8,1,2,4096]{3,2,1,0:T(2,128)S(1)}, f32[8,1,2,4096]{3,2,1,0:T(2,128)S(1)}, u32[]{:S(2)}, u32[]{:S(2)}) collective-permute-start(f32[8,1,2,4096]{3,2,1,0:T(2,128)S(1)} %get-tuple-element.40), channel_id=1, source_target_pairs={{1,0},{2,1},{3,2},{4,3},{5,4},{6,5},{7,6},{8,7},{9,8},{10,9},{11,1... | collective-permute-start | bytes 786440 | tf_op jit(solution)/shard_map/ppermute | solution.py:20
  (52 other events, 284.1 us)
Sparse Core Ops, SparseCore 0:
  33.4 44.7 all-gather.1
where the time goes:
time: 663 us; the launch traced here: 650 us
  matrix products  209 us (32%)
  local copies, waits for them, and re-layouts  188 us (28%)
  blocking collectives  87.9 us (13%)
  starting transfers between devices  57.2 us (9%)
  waiting for transfers between devices  50.9 us (8%)
  other arithmetic  39.8 us (6%)
  between operations  17.4 us (3%)
    dot_general x56, matrix products, block_apply(): return jnp.einsum('abcij,abcjr->abcir', blocks, vector, precision=highest)  205 us
    reshape x48, local copies, waits for them, and re-layouts, faces_sum(): views[face].reshape(vector.shape)  108 us
    ppermute x10, waiting for transfers between devices, extended(): lax.ppermute(lax.slice_in_dim(block, 0, width, axis=dim), axis, backward)  50.8 us
    pmax x1, blocking collectives, local(): upper = lax.pmax(largest_ratio(diag_all, off_all, dof_count), 'grp')  36.2 us
    ppermute x10, starting transfers between devices, extended(): lax.ppermute(lax.slice_in_dim(block, block.shape[dim] - width, None, axis...  34.4 us
    concatenate x17, other arithmetic, extended(): block = jnp.concatenate([low, block, high], axis=dim)  29.8 us
    all_gather x1, blocking collectives, local(): lax.all_gather(coarse_rhs, 'slab', axis=0, tiled=True)  26.6 us
    all_gather x1, blocking collectives, local(): lax.all_gather(own_diag, 'slab', axis=0, tiled=True)  25.1 us
  transfers between devices with their start and end apart: 21, of which 9 were waited for; matrix products, arithmetic and copies ran while one was open for 8% of the time, Pallas kernels for 0%

commit v1 on v0

v1 whole, which is shorter than its diff:
```python
import functools

import jax
import jax.numpy as jnp
from jax import lax
from jax.experimental import pallas as pl
from jax.experimental.pallas import tpu as pltpu
from jax.sharding import PartitionSpec as P

SWEEPS = 8

MESH = pl.DeviceIdType.MESH
f32, bf16 = jnp.float32, jnp.bfloat16
highest = lax.Precision.HIGHEST
DOWN_A, UP_A, DOWN_B, UP_B, DOWN_C, UP_C = range(6)


def split(x):
    hi = x.astype(bf16)
    return hi, (x - hi.astype(f32)).astype(bf16)


def mm(a, b, precision=None):
    return lax.dot_general(
        a, b, (((1,), (0,)), ((), ())), precision=precision, preferred_element_type=f32
    )


def swap_halves(x):
    return pltpu.roll(x, x.shape[-1] // 2, x.ndim - 1)


def kernel(
    slabs,
    grps,
    dens,
    slots,
    neigh,
    codes,
    stiff,
    prolong,
    penalty,
    fine,
    out,
    rho,
    rho_in,
    templ,
    wide,
    own_op,
    far_op,
    rhs,
    resid,
    ijac,
    total,
    w0,
    send,
    from_a,
    from_b,
    top_b,
    top_a,
    final,
    rho_ss,
    rho_rs,
    halo_ss,
    halo_rs,
    topb_ss,
    topb_rs,
    topa_ss,
    topa_rs,
    out_ss,
    out_rs,
    local_sem,
):
    a = lax.axis_index("slab")
    b = lax.axis_index("grp")
    up_a, down_a = lax.rem(a + 1, slabs), lax.rem(a + slabs - 1, slabs)
    up_b, down_b = lax.rem(b + 1, grps), lax.rem(b + grps - 1, grps)

    barrier = pltpu.get_barrier_semaphore()

    def greet_b(d, _):
        pl.semaphore_signal(
            barrier, inc=1, device_id=(a, lax.rem(b + d, grps)), device_id_type=MESH
        )
        return 0

    def greet_a(d, _):
        pl.semaphore_signal(
            barrier, inc=1, device_id=(lax.rem(a + d, slabs), b), device_id_type=MESH
        )
        return 0

    lax.fori_loop(1, grps, greet_b, 0)
    lax.fori_loop(1, slabs, greet_a, 0)

    left = lax.broadcasted_iota(jnp.int32, (64, 128), 1) < 64

    for l in range(4):
        mean = dens[0, l // 2, l % 2, 0]
        for c in range(1, 8):
            mean = mean + dens[0, l // 2, l % 2, c]
        rho[l : l + 1, :] = jnp.full((1, 128), mean * 0.125, f32)
    rho[4:8, :] = jnp.ones((4, 128), f32)

    pl.semaphore_wait(barrier, grps - 1 + slabs - 1)

    def rho_copy(i, to_a, to_b):
        return pltpu.make_async_remote_copy(
            src_ref=rho,
            dst_ref=rho_in.at[i],
            send_sem=rho_ss.at[i],
            recv_sem=rho_rs.at[i],
            device_id=(to_a, to_b),
            device_id_type=MESH,
        )

    rho_copies = [
        rho_copy(DOWN_A, up_a, b),
        rho_copy(UP_A, down_a, b),
        rho_copy(DOWN_B, a, up_b),
        rho_copy(UP_B, a, down_b),
    ]
    for copy in rho_copies:
        copy.start()

    for s in range(8):
        p = prolong[s]
        kp = mm(stiff[...], p, highest)
        templ[s] = mm(p.T, kp, highest)

    for h in range(2):
        for s in range(8):
            wide[pl.ds(s * 32, 32), h * 64 : h * 64 + 64] = prolong[
                s, pl.ds(h, 32, stride=2), :
            ]
    w_hi, w_lo = split(wide[...].T)
    w_both = jnp.concatenate([w_hi, w_lo], axis=0)
    row = lax.broadcasted_iota(jnp.int32, (256, 256), 0)
    col = lax.broadcasted_iota(jnp.int32, (256, 256), 1)
    same_pair = lax.rem(row, 32) == col // 8
    lane = lax.rem(lax.broadcasted_iota(jnp.int32, (1, 256), 1), 8)
    parts = []
    for l in range(4):
        slot_of = jnp.zeros((1, 256), jnp.int32)
        for c in range(8):
            slot_of = jnp.where(lane == c, slots[0, l // 2, l % 2, c], slot_of)
        pick = jnp.where(same_pair & (row // 32 == slot_of), 1.0, 0.0).astype(bf16)
        ordered = mm(pick, fine[l]).astype(bf16)
        both = mm(w_both, ordered)
        parts.append(both[:128] + both[128:])
    for m in range(2):
        y0, y1 = parts[2 * m], parts[2 * m + 1]
        rhs[m] = jnp.where(left, y0[:64], y1[64:]) + swap_halves(
            jnp.where(left, y1[:64], y0[64:])
        )

    for copy in rho_copies:
        copy.wait()
    eye = lax.broadcasted_iota(jnp.int32, (64, 64), 0) == lax.broadcasted_iota(
        jnp.int32, (64, 64), 1
    )
    top = jnp.zeros((1, 1), f32)
    for m in range(2):
        jacs = []
        for k in range(2):
            l = 2 * m + k
            mine = rho[l : l + 1, :]
            faces = {
                DOWN_A: rho_in[DOWN_A, l : l + 1, :],
                UP_A: rho_in[UP_A, l : l + 1, :],
                DOWN_B: rho_in[DOWN_B, 2 + k : 3 + k, :] if m == 0 else rho[k : k + 1, :],
                UP_B: rho[2 + k : 3 + k, :] if m == 0 else rho_in[UP_B, k : k + 1, :],
                (UP_C if k == 0 else DOWN_C): rho[2 * m + 1 - k : 2 * m + 2 - k, :],
            }
            diag = jnp.zeros((64, 64), f32)
            for c in range(8):
                weight = 1.0 / jnp.full((1, 64), dens[0, m, k, c], f32)
                diag = diag + weight * templ[slots[0, m, k, c]]
            offs = {}
            extent = jnp.zeros((64, 64), f32)
            for face, other in faces.items():
                present = (neigh[0, m, k, face] >= 0).astype(f32)
                weight = (2.0 / (mine + other) * present)[:, :64]
                block = weight * penalty[codes[0, m, k, face]]
                diag = diag + block
                extent = extent + jnp.abs(block)
                offs[face] = -block
            jac = jnp.sum(jnp.where(eye, diag, 0.0), axis=1, keepdims=True)
            sums = jnp.sum(jnp.abs(diag) + extent, axis=1, keepdims=True)
            top = jnp.maximum(top, jnp.max(sums / jac, axis=0, keepdims=True))
            jacs.append(1.0 / jac)
            in_pair = UP_B if m == 0 else DOWN_B
            out_pair = DOWN_B if m == 0 else UP_B
            in_c = UP_C if k == 0 else DOWN_C
            for op, three in (
                (own_op, (diag, offs[in_pair], offs[in_c])),
                (far_op, (offs[DOWN_A], offs[UP_A], offs[out_pair])),
            ):
                for at, width, value in (
                    (0, 128, jnp.concatenate(three[:2], axis=1)),
                    (128, 64, three[2]),
                ):
                    hi, lo = split(value)
                    op[m, k * 64 : k * 64 + 64, at : at + width] = hi
                    op[m, 128 + k * 64 : 192 + k * 64, at : at + width] = lo
        ijac[m] = jnp.where(left, jacs[0], jacs[1])

    top_b[0] = jnp.broadcast_to(top, (8, 128))

    def topb_copy(d):
        return pltpu.make_async_remote_copy(
            src_ref=top_b.at[0],
            dst_ref=top_b.at[d],
            send_sem=topb_ss.at[d],
            recv_sem=topb_rs.at[d],
            device_id=(a, lax.rem(b + d, grps)),
            device_id_type=MESH,
        )

    def topa_copy(d):
        return pltpu.make_async_remote_copy(
            src_ref=top_a.at[0],
            dst_ref=top_a.at[d],
            send_sem=topa_ss.at[d],
            recv_sem=topa_rs.at[d],
            device_id=(lax.rem(a + d, slabs), b),
            device_id_type=MESH,
        )

    def each(count, act):
        def body(d, _):
            act(d)
            return 0

        lax.fori_loop(1, count, body, 0)

    def halo(p):
        def copy(i, src, dst, to_a, to_b):
            return pltpu.make_async_remote_copy(
                src_ref=src,
                dst_ref=dst,
                send_sem=halo_ss.at[p, i],
                recv_sem=halo_rs.at[p, i],
                device_id=(to_a, to_b),
                device_id_type=MESH,
            )

        return [
            copy(0, send.at[p], from_a.at[p, 0], up_a, b),
            copy(1, send.at[p], from_a.at[p, 1], down_a, b),
            copy(2, send.at[p, 1], from_b.at[p, 0], a, up_b),
            copy(3, send.at[p, 0], from_b.at[p, 1], a, down_b),
        ]

    def product(op, m, stack):
        hi, lo = split(stack)
        one = mm(op[m], hi)
        return one[:128] + one[128:] + mm(op[m, :128, :], lo)

    def apply(p, copies):
        u = [send[p, 0], send[p, 1]]
        near = [
            product(own_op, m, jnp.concatenate([u[m], u[1 - m], swap_halves(u[m])], axis=0))
            for m in range(2)
        ]
        for copy in copies:
            copy.wait()
        result = []
        for m in range(2):
            stack = jnp.concatenate(
                [from_a[p, 0, m], from_a[p, 1, m], from_b[p, m]], axis=0
            )
            both = near[m] + product(far_op, m, stack)
            result.append(jnp.where(left, both[:64], both[64:]))
        return result

    each(grps, lambda d: topb_copy(d).start())
    copies = halo(0)
    for m in range(2):
        send[0, m] = rhs[m] * ijac[m]
    for copy in copies:
        copy.start()
    first = apply(0, copies)
    each(grps, lambda d: topb_copy(d).wait())
    top_a[0] = jnp.max(top_b[...], axis=0)
    each(slabs, lambda d: topa_copy(d).start())
    copies = halo(1)
    for m in range(2):
        w0[m] = first[m]
        send[1, m] = first[m] * ijac[m]
    for copy in copies:
        copy.start()
    second = apply(1, copies)
    each(slabs, lambda d: topa_copy(d).wait())
    upper = jnp.max(top_a[...], axis=0)[0:1, :]

    lower = upper / 10.0
    centre_val = 0.5 * (upper + lower)
    half_width = 0.5 * (upper - lower)
    sigma = centre_val / half_width
    over_centre = 1.0 / centre_val
    damp0 = 1.0 / sigma
    damp1 = 1.0 / (2.0 * sigma - damp0)
    keep1, gain1 = damp1 * damp0, 2.0 * damp1 / half_width
    damp2 = 1.0 / (2.0 * sigma - damp1)
    keep2, gain2 = damp2 * damp1, 2.0 * damp2 / half_width
    for m in range(2):
        update0 = send[0, m] * over_centre
        resid1 = rhs[m] - w0[m] * over_centre
        update1 = keep1 * update0 + gain1 * (resid1 * ijac[m])
        applied = (keep1 * over_centre) * w0[m] + gain1 * (w0[m] - over_centre * second[m])
        resid2 = resid1 - applied
        update2 = keep2 * update1 + gain2 * (resid2 * ijac[m])
        resid[m] = resid2
        total[m] = update0 + update1 + update2
        send[0, m] = update2

    def sweep(i, damp):
        p = lax.rem(i, 2)
        copies = halo(p)
        for copy in copies:
            copy.start()
        applied = apply(p, copies)
        damp_next = 1.0 / (2.0 * sigma - damp)
        keep, gain = damp_next * damp, 2.0 * damp_next / half_width
        for m in range(2):
            now = resid[m] - applied[m]
            resid[m] = now
            update = keep * send[p, m] + gain * (now * ijac[m])
            total[m] = total[m] + update
            send[1 - p, m] = update
        return damp_next

    lax.fori_loop(0, SWEEPS - 2, sweep, damp2)

    even = lax.rem(lax.broadcasted_iota(jnp.int32, (64, 128), 0), 2) == 0
    for m in range(2):
        x = total[m]
        turned = swap_halves(x)
        moved = jnp.where(even, pltpu.roll(turned, 63, 0), pltpu.roll(turned, 1, 0))
        final[m] = jnp.where(even == left, x, moved)

    def out_copy(d):
        return pltpu.make_async_remote_copy(
            src_ref=final,
            dst_ref=out.at[a],
            send_sem=out_ss.at[d],
            recv_sem=out_rs.at[d],
            device_id=(lax.rem(a + d, slabs), b),
            device_id_type=MESH,
        )

    each(slabs, lambda d: out_copy(d).start())
    keep_own = pltpu.make_async_copy(final, out.at[a], local_sem)
    keep_own.start()
    keep_own.wait()
    each(slabs, lambda d: out_copy(d).wait())


def local(slabs, grps, dens, slots, neigh, codes, stiff, prolong, penalty, fine):
    x = fine.reshape(4, 8, 32, 128).transpose(0, 2, 1, 3).reshape(4, 256, 128)
    smem = pl.BlockSpec(memory_space=pltpu.SMEM)
    vmem = pl.BlockSpec(memory_space=pltpu.VMEM)
    dma = pltpu.SemaphoreType.DMA
    result = pl.pallas_call(
        functools.partial(kernel, slabs, grps),
        out_shape=jax.ShapeDtypeStruct((slabs, 2, 64, 128), f32),
        in_specs=[smem] * 4 + [vmem] * 4,
        out_specs=pl.BlockSpec(memory_space=pl.ANY),
        scratch_shapes=[
            pltpu.VMEM((8, 128), f32),
            pltpu.VMEM((4, 8, 128), f32),
            pltpu.VMEM((8, 64, 64), f32),
            pltpu.VMEM((256, 128), f32),
            pltpu.VMEM((2, 256, 192), bf16),
            pltpu.VMEM((2, 256, 192), bf16),
            pltpu.VMEM((2, 64, 128), f32),
            pltpu.VMEM((2, 64, 128), f32),
            pltpu.VMEM((2, 64, 128), f32),
            pltpu.VMEM((2, 64, 128), f32),
            pltpu.VMEM((2, 64, 128), f32),
            pltpu.VMEM((2, 2, 64, 128), f32),
            pltpu.VMEM((2, 2, 2, 64, 128), f32),
            pltpu.VMEM((2, 2, 64, 128), f32),
            pltpu.VMEM((grps, 8, 128), f32),
            pltpu.VMEM((slabs, 8, 128), f32),
            pltpu.VMEM((2, 64, 128), f32),
            dma((4,)),
            dma((4,)),
            dma((2, 4)),
            dma((2, 4)),
            dma((grps,)),
            dma((grps,)),
            dma((slabs,)),
            dma((slabs,)),
            dma((slabs,)),
            dma((slabs,)),
            dma,
        ],
        compiler_params=pltpu.CompilerParams(
            collective_id=0, has_side_effects=True, vmem_limit_bytes=32 * 2**20
        ),
    )(dens, slots, neigh, codes, stiff, prolong, penalty, x)
    spread = result.reshape(slabs, 2, 32, 2, 128).transpose(0, 1, 3, 2, 4)
    return spread.reshape(slabs, 2, 2, 4096)


def solution(mesh):
    return jax.shard_map(
        functools.partial(local, mesh.shape["slab"], mesh.shape["grp"]),
        mesh=mesh,
        in_specs=(
            P("slab", "grp", None, None),
            P("slab", "grp", None, None),
            P("slab", "grp", None, None),
            P("slab", "grp", None, None),
            P(),
            P(),
            P(),
            P("slab", "grp", None, None, None),
        ),
        out_specs=P(None, "grp", None, None),
        check_vma=False,
    )
```

time: 663 us -> 70.7 us (0.11)
  the two profiles are of different devices: /device:TPU:121 before, /device:TPU:24 now
where the time goes in v1:
time: 70.7 us; the launch traced here: 70.3 us
  Pallas kernels  63.1 us (89%)
  local copies, waits for them, and re-layouts  7.22 us (10%)
    pallas_call x1, Pallas kernels, local(): pl.pallas_call(functools.partial(kernel, slabs, grps), out_shape=jax.Shap...  63.1 us
    unnamed x17, local copies, waits for them, and re-layouts  7.22 us

profile of v1, /device:TPU:24, one launch (start us, length us, event | category | flops | bytes accessed | tf_op | source)
XLA Modules:
  0.0 70.3 jit_solution(903676796874826606)
XLA Ops:
  0.0 0.0 copy-start
  0.0 1.0 %copy-done = f32[16,64,64]{2,1,0:T(8,128)S(1)} copy-done((f32[16,64,64]{2,1,0:T(8,128)S(1)}, f32[16,64,64]{2,1,0:T(8,128)}, u32[]{:S(2)}) %copy-start) | copy-done | bytes 262168
  1.0 0.0 copy-start.1
  1.0 0.9 %copy-done.1 = f32[8,64,64]{2,1,0:T(8,128)S(1)} copy-done((f32[8,64,64]{2,1,0:T(8,128)S(1)}, f32[8,64,64]{2,1,0:T(8,128)}, u32[]{:S(2)}) %copy-start.1) | copy-done | bytes 131096
  2.0 0.0 copy-start.2
  2.0 0.9 %copy-done.2 = bf16[1,2,2,8,4096]{4,3,2,1,0:T(8,128)(2,1)S(1)} copy-done((bf16[1,2,2,8,4096]{4,3,2,1,0:T(8,128)(2,1)S(1)}, bf16[1,2,2,8,4096]{4,3,2,1,0:T(8,128)(2,1)}, u32[]{:S(2)}) %copy-start.2) | copy-done | bytes 262168
  2.9 0.0 copy-start.3
  2.9 0.8 %copy-done.3 = f32[64,64]{1,0:T(8,128)S(1)} copy-done((f32[64,64]{1,0:T(8,128)S(1)}, f32[64,64]{1,0:T(8,128)}, u32[]{:S(2)}) %copy-start.3) | copy-done | bytes 16408
  3.7 0.0 copy-start.4
  3.7 0.7 copy-done.4
  4.4 0.0 copy-start.5
  4.4 0.7 copy-done.5
  5.1 0.0 copy-start.6
  5.1 0.7 copy-done.6
  5.7 0.0 copy-start.7
  5.8 0.7 copy-done.7
  6.4 63.1 %shard_map.82 = f32[8,2,64,128]{3,2,1,0:T(8,128)S(1)} custom-call(f32[1,2,2,8]{3,2,1,0:T(2,128)S(1)} %copy-done.4, s32[1,2,2,8]{3,2,1,0:T(2,128)S(1)} %copy-done.5, s32[1,2,2,6]{3,2,1,0:T(2,128)S(1)} %copy-done.6, s32[1,2,2,6]{3,2,1,0:T(2,128)S(1)} %copy-done.7, f32[64,64]{1,0:T(8,128)S(1)} %copy-done.3, f32[8,64,64]{2,1,0:T(8,128)S(1)} %copy-done.1, ...), custom_call_target="tpu_custom_call" | custom-call | tf_op jit(solution)/shard_map/pallas_call | solution.py:365
  69.5 0.8 %copy.11 = f32[8,2,2,4096]{3,2,1,0:T(2,128)} copy(f32[8,2,2,4096]{3,2,1,0:T(2,128)S(1)} %bitcast.10) | data formatting | bytes 1048576
Async XLA Ops:
  0.0 1.0 %copy-start = (f32[16,64,64]{2,1,0:T(8,128)S(1)}, f32[16,64,64]{2,1,0:T(8,128)}, u32[]{:S(2)}) copy-start(f32[16,64,64]{2,1,0:T(8,128)} %penalty.1) | copy-start | bytes 786436
  1.0 0.9 %copy-start.1 = (f32[8,64,64]{2,1,0:T(8,128)S(1)}, f32[8,64,64]{2,1,0:T(8,128)}, u32[]{:S(2)}) copy-start(f32[8,64,64]{2,1,0:T(8,128)} %prolong.1) | copy-start | bytes 393220
  2.0 0.9 %copy-start.2 = (bf16[1,2,2,8,4096]{4,3,2,1,0:T(8,128)(2,1)S(1)}, bf16[1,2,2,8,4096]{4,3,2,1,0:T(8,128)(2,1)}, u32[]{:S(2)}) copy-start(bf16[1,2,2,8,4096]{4,3,2,1,0:T(8,128)(2,1)} %param.15) | copy-start | bytes 786436
  2.9 0.8 %copy-start.3 = (f32[64,64]{1,0:T(8,128)S(1)}, f32[64,64]{1,0:T(8,128)}, u32[]{:S(2)}) copy-start(f32[64,64]{1,0:T(8,128)} %stiff.1) | copy-start | bytes 49156
  3.7 0.7 copy-start.4
  4.4 0.7 copy-start.5
  5.1 0.7 copy-start.6
  5.7 0.7 copy-start.7

commit v2 on v1

--- a/solution.py
+++ b/solution.py
@@ -33,6 +33,15 @@
 def kernel(
     slabs,
     grps,
+    dens_hbm,
+    slots_hbm,
+    neigh_hbm,
+    codes_hbm,
+    stiff_hbm,
+    prolong_hbm,
+    penalty_hbm,
+    fine_hbm,
+    out,
     dens,
     slots,
     neigh,
@@ -41,7 +50,7 @@
     prolong,
     penalty,
     fine,
-    out,
+    in_sems,
     rho,
     rho_in,
     templ,
@@ -76,6 +85,24 @@
     up_a, down_a = lax.rem(a + 1, slabs), lax.rem(a + slabs - 1, slabs)
     up_b, down_b = lax.rem(b + 1, grps), lax.rem(b + grps - 1, grps)
 
+    dens_in, slots_in, neigh_in, codes_in, stiff_in, prolong_in, penalty_in, fine_in = loads = [
+        pltpu.make_async_copy(src, dst, in_sems.at[i])
+        for i, (src, dst) in enumerate(
+            (
+                (dens_hbm, dens),
+                (slots_hbm, slots),
+                (neigh_hbm, neigh),
+                (codes_hbm, codes),
+                (stiff_hbm, stiff),
+                (prolong_hbm, prolong),
+                (penalty_hbm, penalty),
+                (fine_hbm, fine),
+            )
+        )
+    ]
+    for load in loads:
+        load.start()
+
     barrier = pltpu.get_barrier_semaphore()
 
     def greet_b(d, _):
@@ -95,6 +122,7 @@
 
     left = lax.broadcasted_iota(jnp.int32, (64, 128), 1) < 64
 
+    dens_in.wait()
     for l in range(4):
         mean = dens[0, l // 2, l % 2, 0]
         for c in range(1, 8):
@@ -123,6 +151,8 @@
     for copy in rho_copies:
         copy.start()
 
+    stiff_in.wait()
+    prolong_in.wait()
     for s in range(8):
         p = prolong[s]
         kp = mm(stiff[...], p, highest)
@@ -140,6 +170,8 @@
     same_pair = lax.rem(row, 32) == col // 8
     lane = lax.rem(lax.broadcasted_iota(jnp.int32, (1, 256), 1), 8)
     parts = []
+    slots_in.wait()
+    fine_in.wait()
     for l in range(4):
         slot_of = jnp.zeros((1, 256), jnp.int32)
         for c in range(8):
@@ -154,6 +186,9 @@
             jnp.where(left, y1[:64], y0[64:])
         )
 
+    neigh_in.wait()
+    codes_in.wait()
+    penalty_in.wait()
     for copy in rho_copies:
         copy.wait()
     eye = lax.broadcasted_iota(jnp.int32, (64, 64), 0) == lax.broadcasted_iota(
@@ -359,15 +394,17 @@
 
 def local(slabs, grps, dens, slots, neigh, codes, stiff, prolong, penalty, fine):
     x = fine.reshape(4, 8, 32, 128).transpose(0, 2, 1, 3).reshape(4, 256, 128)
-    smem = pl.BlockSpec(memory_space=pltpu.SMEM)
-    vmem = pl.BlockSpec(memory_space=pltpu.VMEM)
+    smem, vmem = pltpu.SMEM, pltpu.VMEM
+    args = (dens, slots, neigh, codes, stiff, prolong, penalty, x)
     dma = pltpu.SemaphoreType.DMA
     result = pl.pallas_call(
         functools.partial(kernel, slabs, grps),
         out_shape=jax.ShapeDtypeStruct((slabs, 2, 64, 128), f32),
-        in_specs=[smem] * 4 + [vmem] * 4,
+        in_specs=[pl.BlockSpec(memory_space=pl.ANY)] * 8,
         out_specs=pl.BlockSpec(memory_space=pl.ANY),
         scratch_shapes=[
+            *(space(v.shape, v.dtype) for space, v in zip([smem] * 4 + [vmem] * 4, args)),
+            dma((8,)),
             pltpu.VMEM((8, 128), f32),
             pltpu.VMEM((4, 8, 128), f32),
             pltpu.VMEM((8, 64, 64), f32),
@@ -398,9 +435,9 @@
             dma,
         ],
         compiler_params=pltpu.CompilerParams(
-            collective_id=0, has_side_effects=True, vmem_limit_bytes=32 * 2**20
+            collective_id=0, has_side_effects=True
         ),
-    )(dens, slots, neigh, codes, stiff, prolong, penalty, x)
+    )(*args)
     spread = result.reshape(slabs, 2, 32, 2, 128).transpose(0, 1, 3, 2, 4)
     return spread.reshape(slabs, 2, 2, 4096)
 

time: 70.7 us -> 64.6 us (0.914)
  local copies, waits for them, and re-layouts: 7.22 us -> 1.89 us
    unnamed x17 -> x1, local copies, waits for them, and re-layouts: 7.22 us -> 1.89 us
where the time goes in v2:
time: 64.6 us; the launch traced here: 64.5 us
  Pallas kernels  62.6 us (97%)
  local copies, waits for them, and re-layouts  1.89 us (3%)
    pallas_call x1, Pallas kernels, local(): pl.pallas_call(functools.partial(kernel, slabs, grps), out_shape=jax.Shap...  62.6 us
    unnamed x1, local copies, waits for them, and re-layouts  1.89 us

profile of v2, /device:TPU:24, one launch (start us, length us, event | category | flops | bytes accessed | tf_op | source)
XLA Modules:
  0.0 64.5 jit_solution(2089045691869706485)
XLA Ops:
  0.0 62.6 %shard_map.82 = f32[8,2,64,128]{3,2,1,0:T(8,128)} custom-call(f32[1,2,2,8]{3,2,1,0:T(2,128)} %dens_hbm.1, s32[1,2,2,8]{3,2,1,0:T(2,128)} %slots_hbm.1, s32[1,2,2,6]{3,2,1,0:T(2,128)} %neigh_hbm.1, s32[1,2,2,6]{3,2,1,0:T(2,128)} %codes_hbm.1, f32[64,64]{1,0:T(8,128)} %stiff_hbm.1, f32[8,64,64]{2,1,0:T(8,128)} %prolong_hbm.1, f32[16,64,64]{2,1,0:T(8,128)} %penalty_hbm.1, ...), custom_call_target="tpu_custom_call" | custom-call | tf_op jit(solution)/shard_map/pallas_call | solution.py:400
  62.6 1.9 %copy.11 = f32[8,2,2,4096]{3,2,1,0:T(2,128)} copy(f32[8,2,2,4096]{3,2,1,0:T(2,128)} %bitcast.10) | data formatting | bytes 1048576

commit v3 on v2

v3 whole, which is shorter than its diff:
```python
import functools

import jax
import jax.numpy as jnp
from jax import lax
from jax.experimental import pallas as pl
from jax.experimental.pallas import tpu as pltpu
from jax.sharding import PartitionSpec as P

SWEEPS = 8
UNITS = SWEEPS + 2
REACH = SWEEPS // 4

MESH = pl.DeviceIdType.MESH
f32, bf16 = jnp.float32, jnp.bfloat16
highest = lax.Precision.HIGHEST
DOWN_A, UP_A, DOWN_B, UP_B, DOWN_C, UP_C = range(6)


def split(x):
    hi = x.astype(bf16)
    return hi, (x - hi.astype(f32)).astype(bf16)


def mm(a, b, precision=None, across=0):
    return lax.dot_general(
        a, b, (((1,), (across,)), ((), ())), precision=precision, preferred_element_type=f32
    )


def roll(x, by):
    return pltpu.roll(x, by % 128, 1)


def iota(shape, dim):
    return lax.broadcasted_iota(jnp.int32, shape, dim)


def kernel(
    slabs,
    grps,
    dens_hbm,
    slots_hbm,
    neigh_hbm,
    codes_hbm,
    stiff_hbm,
    prolong_hbm,
    penalty_hbm,
    fine_hbm,
    out,
    dens,
    slots,
    neigh,
    codes,
    stiff,
    prolong,
    penalty,
    fine,
    in_sems,
    rho,
    rho_in,
    templ,
    wide,
    ops,
    pack,
    held,
    weights,
    rhs,
    ijac,
    vec,
    part,
    g_up,
    g_down,
    w0,
    resid,
    total,
    top_1,
    top_2,
    done,
    parts,
    rho_ss,
    rho_rs,
    held_ss,
    held_rs,
    top1_ss,
    top1_rs,
    top2_ss,
    top2_rs,
    parts_ss,
    parts_rs,
):
    chunks = 2 * slabs
    q = 64 // chunks
    rows = 2 * q
    pairs = grps // 2
    a = lax.axis_index("slab")
    b = lax.axis_index("grp")
    core = lax.rem(b, 2)
    pair = b // 2
    mine = 2 * a + core
    up_a, down_a = lax.rem(a + 1, slabs), lax.rem(a + slabs - 1, slabs)
    up_b, down_b = lax.rem(b + 1, grps), lax.rem(b + grps - 1, grps)

    loads = [
        pltpu.make_async_copy(src, dst, in_sems.at[i])
        for i, (src, dst) in enumerate(
            (
                (dens_hbm, dens),
                (slots_hbm, slots),
                (neigh_hbm, neigh),
                (codes_hbm, codes),
                (stiff_hbm, stiff),
                (prolong_hbm, prolong),
                (penalty_hbm, penalty),
                (fine_hbm, fine),
            )
        )
    ]
    dens_in, slots_in, neigh_in, codes_in, stiff_in, prolong_in, penalty_in, fine_in = loads
    for load in loads:
        load.start()

    def each(first, last, act):
        def body(d, _):
            act(d)
            return 0

        lax.fori_loop(first, last, body, 0)

    def device(step, d):
        chunk = lax.rem(mine + d, chunks)
        return chunk, (chunk // 2, 2 * lax.rem(pair + step + pairs, pairs) + lax.rem(chunk, 2))

    def along(d):
        return (a, 2 * lax.rem(pair + d, pairs) + core)

    barrier = pltpu.get_barrier_semaphore()

    def greet(where):
        pl.semaphore_signal(barrier, inc=1, device_id=where, device_id_type=MESH)

    steps = [0] + [sign * n for n in range(1, REACH + 1) for sign in (1, -1)]
    for step in steps:
        each(1 if step == 0 else 0, chunks, lambda d: greet(device(step, d)[1]))
    each(REACH + 1, pairs - REACH, lambda d: greet(along(d)))

    left = iota((64, 128), 1) < 64

    dens_in.wait()
    for l in range(4):
        mean = dens[0, l // 2, l % 2, 0]
        for c in range(1, 8):
            mean = mean + dens[0, l // 2, l % 2, c]
        rho[l : l + 1, :] = jnp.full((1, 128), mean * 0.125, f32)
    rho[4:8, :] = jnp.ones((4, 128), f32)

    pl.semaphore_wait(barrier, (2 * REACH + 1) * chunks - 1 + max(0, pairs - 2 * REACH - 1))

    def rho_copy(i, to_a, to_b):
        return pltpu.make_async_remote_copy(
            src_ref=rho,
            dst_ref=rho_in.at[i],
            send_sem=rho_ss.at[i],
            recv_sem=rho_rs.at[i],
            device_id=(to_a, to_b),
            device_id_type=MESH,
        )

    rho_copies = [
        rho_copy(DOWN_A, up_a, b),
        rho_copy(UP_A, down_a, b),
        rho_copy(DOWN_B, a, up_b),
        rho_copy(UP_B, a, down_b),
    ]
    for copy in rho_copies:
        copy.start()

    prolong_in.wait()
    for h in range(2):
        for s in range(8):
            wide[pl.ds(s * 32, 32), h * 64 : h * 64 + 64] = prolong[
                s, pl.ds(h, 32, stride=2), :
            ]
    w_hi, w_lo = split(wide[...].T)
    w_both = jnp.concatenate([w_hi, w_lo], axis=0)
    row, col = iota((256, 256), 0), iota((256, 256), 1)
    same_pair = lax.rem(row, 32) == col // 8
    cell = lax.rem(iota((1, 256), 1), 8)
    slots_in.wait()
    fine_in.wait()
    ys = []
    for l in range(4):
        slot_of = jnp.zeros((1, 256), jnp.int32)
        for c in range(8):
            slot_of = jnp.where(cell == c, slots[0, l // 2, l % 2, c], slot_of)
        pick = jnp.where(same_pair & (row // 32 == slot_of), 1.0, 0.0).astype(bf16)
        ordered = mm(pick, fine[l]).astype(bf16)
        both = mm(w_both, ordered)
        ys.append(both[:128] + both[128:])
    coarse = []
    for m in range(2):
        y0, y1 = ys[2 * m], ys[2 * m + 1]
        coarse.append(
            jnp.where(left, y0[:64], y1[64:]) + roll(jnp.where(left, y1[:64], y0[64:]), 64)
        )
    r128, l128 = iota((128, 128), 0), iota((128, 128), 1)
    order = jnp.where(
        lax.rem(r128 // q, 2) * 64 + (r128 // rows) * q + lax.rem(r128, q) == l128, 1.0, 0.0
    ).astype(bf16)
    hi, lo = split(jnp.concatenate(coarse, axis=0))
    cut = mm(order, hi, across=1) + mm(order, lo, across=1)
    for chunk in range(chunks):
        pack[chunk, :rows, :] = cut[chunk * rows : chunk * rows + rows]

    stiff_in.wait()
    penalty_in.wait()
    eye = iota((64, 64), 0) == iota((64, 64), 1)
    lane64 = iota((64, 128), 1)
    diags = jnp.zeros((64, 128), f32)
    for s in range(24):
        if s < 8:
            p = prolong[s]
            kp = mm(stiff[...], p, highest)
            matrix = mm(p.T, kp, highest)
            templ[s] = matrix
        else:
            matrix = penalty[s - 8]
        column = jnp.sum(jnp.where(eye, matrix, 0.0), axis=1, keepdims=True)
        diags = jnp.where(lane64 == s, column, diags)
        hi, lo = split(matrix)
        two = jnp.concatenate([hi, lo], axis=1)
        for i in range(4):
            ops[i, s * 16 : s * 16 + 16, 0:128] = two[i * 16 : i * 16 + 16]
            ops[i, s * 16 : s * 16 + 16, 128:192] = hi[i * 16 : i * 16 + 16]

    neigh_in.wait()
    codes_in.wait()
    for copy in rho_copies:
        copy.wait()
    lane, half = iota((rows, 128), 1), iota((rows, 128), 0) // q
    tile = jnp.ones((rows, 128), f32)
    face_w = []
    for m in range(2):
        for k in range(2):
            l = 2 * m + k
            own = rho[l : l + 1, :]
            faces = {
                DOWN_A: rho_in[DOWN_A, l : l + 1, :],
                UP_A: rho_in[UP_A, l : l + 1, :],
                DOWN_B: rho_in[DOWN_B, 2 + k : 3 + k, :] if m == 0 else rho[k : k + 1, :],
                UP_B: rho[2 + k : 3 + k, :] if m == 0 else rho_in[UP_B, k : k + 1, :],
                (UP_C if k == 0 else DOWN_C): rho[2 * m + 1 - k : 2 * m + 2 - k, :],
            }
            for c in range(8):
                at = (half == k) & (lane == m * 64 + slots[0, m, k, c])
                tile = jnp.where(at, dens[0, m, k, c], tile)
            face_w.append({})
            for face, other in faces.items():
                present = (neigh[0, m, k, face] >= 0).astype(f32)
                face_w[l][face] = 2.0 / (own + other) * present
    tile = 1.0 / tile
    for m in range(2):
        for k in range(2):
            for face in range(6):
                code = codes[0, m, k, face].astype(f32)
                weight = face_w[2 * m + k].get(face, jnp.zeros((1, 128), f32))
                tile = jnp.where((half == k) & (lane == m * 64 + 8 + face), code, tile)
                tile = jnp.where((half == k) & (lane == m * 64 + 14 + face), weight, tile)
    for chunk in range(chunks):
        pack[chunk, rows:, :] = tile

    def held_copy(n, d):
        chunk, where = device(steps[n], d)
        return pltpu.make_async_remote_copy(
            src_ref=pack.at[chunk],
            dst_ref=held.at[2 * REACH - 2 * steps[n] + core, a],
            send_sem=held_ss.at[n, d],
            recv_sem=held_rs.at[n, d],
            device_id=where,
            device_id_type=MESH,
        )

    for n in reversed(range(len(steps))):
        each(1 if n == 0 else 0, chunks, lambda d: held_copy(n, d).start())
    held[2 * REACH + core, a] = pack[mine]

    top = jnp.zeros((1, 1), f32)
    for m in range(2):
        for k in range(2):
            diag = jnp.zeros((64, 64), f32)
            for c in range(8):
                weight = 1.0 / jnp.full((1, 64), dens[0, m, k, c], f32)
                diag = diag + weight * templ[slots[0, m, k, c]]
            extent = jnp.zeros((64, 64), f32)
            for face, weight in face_w[2 * m + k].items():
                block = weight[:, :64] * penalty[codes[0, m, k, face]]
                diag = diag + block
                extent = extent + jnp.abs(block)
            jac = jnp.sum(jnp.where(eye, diag, 0.0), axis=1, keepdims=True)
            sums = jnp.sum(jnp.abs(diag) + extent, axis=1, keepdims=True)
            top = jnp.maximum(top, jnp.max(sums / jac, axis=0, keepdims=True))

    top_1[0] = jnp.broadcast_to(top, (8, 128))

    def top1_copy(d):
        return pltpu.make_async_remote_copy(
            src_ref=top_1.at[0],
            dst_ref=top_1.at[d],
            send_sem=top1_ss.at[d],
            recv_sem=top1_rs.at[d],
            device_id=device(0, d)[1],
            device_id_type=MESH,
        )

    def top2_copy(d):
        return pltpu.make_async_remote_copy(
            src_ref=top_2.at[0],
            dst_ref=top_2.at[d],
            send_sem=top2_ss.at[d],
            recv_sem=top2_rs.at[d],
            device_id=along(d),
            device_id_type=MESH,
        )

    each(1, chunks, lambda d: top1_copy(d).start())

    for n in range(len(steps)):
        each(1 if n == 0 else 0, chunks, lambda d: held_copy(n, d).wait())
    code16 = iota((16, 128), 0).astype(f32)

    def unpack(j, _):
        got = held[j]
        x = got[:, :rows, :].reshape(64, 128).T
        x = jnp.concatenate([x[:64], x[64:]], axis=1)
        meta = got[:, rows:, :].reshape(64, 128).T
        meta = jnp.concatenate([meta[0:32], meta[64:96]], axis=1)
        weights[j, 0:8, :] = meta[0:8]
        summed = jnp.zeros((16, 128), f32)
        for face in range(6):
            hot = jnp.where(
                code16 == meta[8 + face : 9 + face], meta[14 + face : 15 + face], 0.0
            )
            weights[j, 8 + 16 * face : 24 + 16 * face, :] = hot
            summed = summed + hot
        table = jnp.concatenate([meta[0:8], summed, jnp.zeros((104, 128), f32)], axis=0)
        over = 1.0 / mm(diags, table, highest)
        rhs[j] = x
        ijac[j] = over
        vec[j] = x * over
        return 0

    lax.fori_loop(0, UNITS, unpack, 0)

    each(1, chunks, lambda d: top1_copy(d).wait())
    top_2[0] = jnp.max(top_1[...], axis=0)
    each(1, pairs, lambda d: top2_copy(d).start())

    def products(t):
        def two(i, _):
            j = t // 2 + 2 * i
            hi, lo = split(jnp.concatenate([vec[j], vec[j + 1]], axis=1))
            stack = jnp.concatenate([hi, hi, lo], axis=0)
            for n in range(4):
                every = mm(ops[n], stack)
                at = slice(n * 16, n * 16 + 16)
                for u in range(2):
                    y = every[:, u * 128 : u * 128 + 128]
                    result = jnp.zeros((16, 128), f32)
                    for s in range(8):
                        result = result + weights[j + u, s : s + 1, :] * y[s * 16 : s * 16 + 16]
                    g = []
                    for face in range(6):
                        flux = jnp.zeros((16, 128), f32)
                        for c in range(16):
                            w = 8 + 16 * face + c
                            flux = flux + (
                                weights[j + u, w : w + 1, :] * y[128 + c * 16 : 144 + c * 16]
                            )
                        g.append(flux)
                        result = result + flux
                    result = result - roll(g[UP_A], rows) - roll(g[DOWN_A], -rows)
                    part[j + u, at, :] = result - roll(g[UP_C], q) - roll(g[DOWN_C], -q)
                    g_up[j + u, at, :] = g[UP_B]
                    g_down[j + u, at, :] = g[DOWN_B]
            return 0

        lax.fori_loop(0, SWEEPS // 2 + 1 - t // 2, two, 0)

    def applied(t, use):
        def one(j, _):
            below, above = jnp.maximum(j - 1, 0), jnp.minimum(j + 1, UNITS - 1)
            low = roll(jnp.where(left, g_up[j], g_up[below]), 64)
            high = roll(jnp.where(left, g_down[above], g_down[j]), 64)
            use(j, part[j] - low - high)
            return 0

        lax.fori_loop((t + 1) // 2, UNITS - (t + 1) // 2, one, 0)

    def keep_first(j, value):
        w0[j] = value
        vec[j] = value * ijac[j]

    products(0)
    applied(0, keep_first)
    products(1)
    each(1, pairs, lambda d: top2_copy(d).wait())
    upper = jnp.max(top_2[...], axis=0)[0:1, :]

    lower = upper / 10.0
    centre_val = 0.5 * (upper + lower)
    half_width = 0.5 * (upper - lower)
    sigma = centre_val / half_width
    over_centre = 1.0 / centre_val
    damp0 = 1.0 / sigma
    damp1 = 1.0 / (2.0 * sigma - damp0)
    keep1, gain1 = damp1 * damp0, 2.0 * damp1 / half_width
    damp2 = 1.0 / (2.0 * sigma - damp1)
    keep2, gain2 = damp2 * damp1, 2.0 * damp2 / half_width

    def combine(j, second):
        over, first = ijac[j], w0[j]
        update0 = rhs[j] * over * over_centre
        resid1 = rhs[j] - first * over_centre
        update1 = keep1 * update0 + gain1 * (resid1 * over)
        both = (keep1 * over_centre) * first + gain1 * (first - over_centre * second)
        resid2 = resid1 - both
        update2 = keep2 * update1 + gain2 * (resid2 * over)
        resid[j] = resid2
        total[j] = update0 + update1 + update2
        vec[j] = update2

    applied(1, combine)

    def sweep(t, damp):
        damp_next = 1.0 / (2.0 * sigma - damp)
        keep, gain = damp_next * damp, 2.0 * damp_next / half_width

        def step(j, value):
            now = resid[j] - value
            resid[j] = now
            update = keep * vec[j] + gain * (now * ijac[j])
            total[j] = total[j] + update
            vec[j] = update

        products(t)
        applied(t, step)
        return damp_next

    lax.fori_loop(2, SWEEPS, sweep, damp2)

    for u in range(2):
        x = total[2 * REACH + u]
        done[u] = jnp.concatenate([x[:, :64], x[:, 64:]], axis=0).T

    def parts_copy(d):
        chunk, where = device(0, d)
        return pltpu.make_async_remote_copy(
            src_ref=done.at[lax.rem(chunk, 2)],
            dst_ref=parts.at[mine],
            send_sem=parts_ss.at[d],
            recv_sem=parts_rs.at[d],
            device_id=where,
            device_id_type=MESH,
        )

    each(1, chunks, lambda d: parts_copy(d).start())
    parts[mine] = done[core]
    each(1, chunks, lambda d: parts_copy(d).wait())

    even = lax.rem(iota((64, 128), 0), 2) == 0

    def place(i, _):
        at = pl.ds(pl.multiple_of(i * rows, rows), rows)
        hi, lo = split(parts[:, at, :].reshape(128, 128).T)
        x = mm(hi, order) + mm(lo, order)
        for m in range(2):
            own = x[m * 64 : m * 64 + 64]
            turned = roll(own, 64)
            moved = jnp.where(even, pltpu.roll(turned, 63, 0), pltpu.roll(turned, 1, 0))
            out[i, m] = jnp.where(even == left, own, moved)
        return 0

    lax.fori_loop(0, slabs, place, 0)


def local(slabs, grps, dens, slots, neigh, codes, stiff, prolong, penalty, fine):
    x = fine.reshape(4, 8, 32, 128).transpose(0, 2, 1, 3).reshape(4, 256, 128)
    smem, vmem = pltpu.SMEM, pltpu.VMEM
    args = (dens, slots, neigh, codes, stiff, prolong, penalty, x)
    dma = pltpu.SemaphoreType.DMA
    chunks, pairs = 2 * slabs, grps // 2
    rows = 128 // chunks
    reach = 2 * REACH + 1
    columns = pltpu.VMEM((UNITS, 64, 128), f32)
    result = pl.pallas_call(
        functools.partial(kernel, slabs, grps),
        out_shape=jax.ShapeDtypeStruct((slabs, 2, 64, 128), f32),
        in_specs=[pl.BlockSpec(memory_space=pl.ANY)] * 8,
        out_specs=pl.BlockSpec(memory_space=pltpu.VMEM),
        scratch_shapes=[
            *(space(v.shape, v.dtype) for space, v in zip([smem] * 4 + [vmem] * 4, args)),
            dma((8,)),
            pltpu.VMEM((8, 128), f32),
            pltpu.VMEM((4, 8, 128), f32),
            pltpu.VMEM((8, 64, 64), f32),
            pltpu.VMEM((256, 128), f32),
            pltpu.VMEM((4, 384, 192), bf16),
            pltpu.VMEM((chunks, 2 * rows, 128), f32),
            pltpu.VMEM((UNITS, slabs, 2 * rows, 128), f32),
            pltpu.VMEM((UNITS, 104, 128), f32),
            *[columns] * 9,
            pltpu.VMEM((chunks, 8, 128), f32),
            pltpu.VMEM((pairs, 8, 128), f32),
            pltpu.VMEM((2, 64, 128), f32),
            pltpu.VMEM((chunks, 64, 128), f32),
            dma((4,)),
            dma((4,)),
            dma((reach, chunks)),
            dma((reach, chunks)),
            dma((chunks,)),
            dma((chunks,)),
            dma((pairs,)),
            dma((pairs,)),
            dma((chunks,)),
            dma((chunks,)),
        ],
        compiler_params=pltpu.CompilerParams(collective_id=0, has_side_effects=True),
    )(*args)
    spread = result.reshape(slabs, 2, 32, 2, 128).transpose(0, 1, 3, 2, 4)
    return spread.reshape(slabs, 2, 2, 4096)


def solution(mesh):
    return jax.shard_map(
        functools.partial(local, mesh.shape["slab"], mesh.shape["grp"]),
        mesh=mesh,
        in_specs=(
            P("slab", "grp", None, None),
            P("slab", "grp", None, None),
            P("slab", "grp", None, None),
            P("slab", "grp", None, None),
            P(),
            P(),
            P(),
            P("slab", "grp", None, None, None),
        ),
        out_specs=P(None, "grp", None, None),
        check_vma=False,
    )
```

time: 64.6 us -> 70.8 us (1.096)
  the two profiles are of different devices: /device:TPU:24 before, /device:TPU:1 now
where the time goes in v3:
time: 70.8 us; the launch traced here: 70.7 us
  Pallas kernels  68.8 us (97%)
  local copies, waits for them, and re-layouts  1.89 us (3%)
    pallas_call x1, Pallas kernels, local(): pl.pallas_call(functools.partial(kernel, slabs, grps), out_shape=jax.Shap...  68.8 us
    unnamed x1, local copies, waits for them, and re-layouts  1.89 us

profile of v3, /device:TPU:1, one launch (start us, length us, event | category | flops | bytes accessed | tf_op | source)
XLA Modules:
  0.0 70.7 jit_solution(3064141218729779940)
XLA Ops:
  0.0 68.8 %shard_map.82 = f32[8,2,64,128]{3,2,1,0:T(8,128)} custom-call(f32[1,2,2,8]{3,2,1,0:T(2,128)} %dens_hbm.1, s32[1,2,2,8]{3,2,1,0:T(2,128)} %slots_hbm.1, s32[1,2,2,6]{3,2,1,0:T(2,128)} %neigh_hbm.1, s32[1,2,2,6]{3,2,1,0:T(2,128)} %codes_hbm.1, f32[64,64]{1,0:T(8,128)} %stiff_hbm.1, f32[8,64,64]{2,1,0:T(8,128)} %prolong_hbm.1, f32[16,64,64]{2,1,0:T(8,128)} %penalty_hbm.1, ...), custom_call_target="tpu_custom_call" | custom-call | tf_op jit(solution)/shard_map/pallas_call | solution.py:495
  68.8 1.9 %copy.11 = f32[8,2,2,4096]{3,2,1,0:T(2,128)} copy(f32[8,2,2,4096]{3,2,1,0:T(2,128)} %bitcast.10) | data formatting | bytes 1048576

commit v4 on v3

--- a/solution.py
+++ b/solution.py
@@ -8,8 +8,9 @@
 from jax.sharding import PartitionSpec as P
 
 SWEEPS = 8
-UNITS = SWEEPS + 2
-REACH = SWEEPS // 4
+REACH = 1
+SPAN = 4 * REACH
+UNITS = 4 * REACH + 2
 
 MESH = pl.DeviceIdType.MESH
 f32, bf16 = jnp.float32, jnp.bfloat16
@@ -76,6 +77,8 @@
     total,
     top_1,
     top_2,
+    edge,
+    edge_in,
     done,
     parts,
     rho_ss,
@@ -86,6 +89,8 @@
     top1_rs,
     top2_ss,
     top2_rs,
+    edge_ss,
+    edge_rs,
     parts_ss,
     parts_rs,
 ):
@@ -229,9 +234,9 @@
         diags = jnp.where(lane64 == s, column, diags)
         hi, lo = split(matrix)
         two = jnp.concatenate([hi, lo], axis=1)
-        for i in range(4):
-            ops[i, s * 16 : s * 16 + 16, 0:128] = two[i * 16 : i * 16 + 16]
-            ops[i, s * 16 : s * 16 + 16, 128:192] = hi[i * 16 : i * 16 + 16]
+        for i in range(2):
+            ops[i, s * 32 : s * 32 + 32, 0:128] = two[i * 32 : i * 32 + 32]
+            ops[i, s * 32 : s * 32 + 32, 128:192] = hi[i * 32 : i * 32 + 32]
 
     neigh_in.wait()
     codes_in.wait()
@@ -334,14 +339,12 @@
         x = jnp.concatenate([x[:64], x[64:]], axis=1)
         meta = got[:, rows:, :].reshape(64, 128).T
         meta = jnp.concatenate([meta[0:32], meta[64:96]], axis=1)
-        weights[j, 0:8, :] = meta[0:8]
+        weights[j] = meta
         summed = jnp.zeros((16, 128), f32)
         for face in range(6):
-            hot = jnp.where(
+            summed = summed + jnp.where(
                 code16 == meta[8 + face : 9 + face], meta[14 + face : 15 + face], 0.0
             )
-            weights[j, 8 + 16 * face : 24 + 16 * face, :] = hot
-            summed = summed + hot
         table = jnp.concatenate([meta[0:8], summed, jnp.zeros((104, 128), f32)], axis=0)
         over = 1.0 / mm(diags, table, highest)
         rhs[j] = x
@@ -360,31 +363,30 @@
             j = t // 2 + 2 * i
             hi, lo = split(jnp.concatenate([vec[j], vec[j + 1]], axis=1))
             stack = jnp.concatenate([hi, hi, lo], axis=0)
-            for n in range(4):
+            for n in range(2):
                 every = mm(ops[n], stack)
-                at = slice(n * 16, n * 16 + 16)
+                at = slice(n * 32, n * 32 + 32)
                 for u in range(2):
                     y = every[:, u * 128 : u * 128 + 128]
-                    result = jnp.zeros((16, 128), f32)
-                    for s in range(8):
-                        result = result + weights[j + u, s : s + 1, :] * y[s * 16 : s * 16 + 16]
+                    w = weights.at[j + u]
+                    result = w[0:1, :] * y[0:32]
+                    for s in range(1, 8):
+                        result = result + w[s : s + 1, :] * y[s * 32 : s * 32 + 32]
                     g = []
                     for face in range(6):
-                        flux = jnp.zeros((16, 128), f32)
-                        for c in range(16):
-                            w = 8 + 16 * face + c
-                            flux = flux + (
-                                weights[j + u, w : w + 1, :] * y[128 + c * 16 : 144 + c * 16]
-                            )
-                        g.append(flux)
-                        result = result + flux
+                        code = jnp.broadcast_to(w[8 + face : 9 + face, :], (32, 128))
+                        flux = y[256:288]
+                        for c in range(1, 16):
+                            flux = jnp.where(code == c, y[256 + c * 32 : 288 + c * 32], flux)
+                        g.append(w[14 + face : 15 + face, :] * flux)
+                        result = result + g[face]
                     result = result - roll(g[UP_A], rows) - roll(g[DOWN_A], -rows)
                     part[j + u, at, :] = result - roll(g[UP_C], q) - roll(g[DOWN_C], -q)
                     g_up[j + u, at, :] = g[UP_B]
                     g_down[j + u, at, :] = g[DOWN_B]
             return 0
 
-        lax.fori_loop(0, SWEEPS // 2 + 1 - t // 2, two, 0)
+        lax.fori_loop(0, UNITS // 2 - t // 2, two, 0)
 
     def applied(t, use):
         def one(j, _):
@@ -446,7 +448,30 @@
         applied(t, step)
         return damp_next
 
-    lax.fori_loop(2, SWEEPS, sweep, damp2)
+    damp = lax.fori_loop(2, SPAN, sweep, damp2)
+
+    edge[0] = vec[2 * REACH : 2 * REACH + 2]
+    edge[1] = resid[2 * REACH : 2 * REACH + 2]
+
+    def edge_copy(side, d):
+        return pltpu.make_async_remote_copy(
+            src_ref=edge,
+            dst_ref=edge_in.at[side],
+            send_sem=edge_ss.at[side],
+            recv_sem=edge_rs.at[side],
+            device_id=along(d),
+            device_id_type=MESH,
+        )
+
+    edge_copies = [edge_copy(0, 1), edge_copy(1, pairs - 1)]
+    for copy in edge_copies:
+        copy.start()
+    for copy in edge_copies:
+        copy.wait()
+    for side in range(2):
+        vec[4 * side : 4 * side + 2] = edge_in[side, 0]
+        resid[4 * side : 4 * side + 2] = edge_in[side, 1]
+    lax.fori_loop(0, SWEEPS - SPAN, sweep, damp)
 
     for u in range(2):
         x = total[2 * REACH + u]
@@ -504,13 +529,15 @@
             pltpu.VMEM((4, 8, 128), f32),
             pltpu.VMEM((8, 64, 64), f32),
             pltpu.VMEM((256, 128), f32),
-            pltpu.VMEM((4, 384, 192), bf16),
+            pltpu.VMEM((2, 768, 192), bf16),
             pltpu.VMEM((chunks, 2 * rows, 128), f32),
             pltpu.VMEM((UNITS, slabs, 2 * rows, 128), f32),
-            pltpu.VMEM((UNITS, 104, 128), f32),
+            pltpu.VMEM((UNITS, 32, 128), f32),
             *[columns] * 9,
             pltpu.VMEM((chunks, 8, 128), f32),
             pltpu.VMEM((pairs, 8, 128), f32),
+            pltpu.VMEM((2, 2, 64, 128), f32),
+            pltpu.VMEM((2, 2, 2, 64, 128), f32),
             pltpu.VMEM((2, 64, 128), f32),
             pltpu.VMEM((chunks, 64, 128), f32),
             dma((4,)),
@@ -521,6 +548,8 @@
             dma((chunks,)),
             dma((pairs,)),
             dma((pairs,)),
+            dma((2,)),
+            dma((2,)),
             dma((chunks,)),
             dma((chunks,)),
         ],

time: 70.8 us -> 60.7 us (0.86)
  Pallas kernels: 68.8 us -> 58.7 us
    pallas_call x1, Pallas kernels: 68.8 us -> 58.7 us  [local(): pl.pallas_call(functools.partial(kernel, slabs, grps), out_shape=jax.Shap...]
where the time goes in v4:
time: 60.7 us; the launch traced here: 60.6 us
  Pallas kernels  58.7 us (97%)
  local copies, waits for them, and re-layouts  1.89 us (3%)
    pallas_call x1, Pallas kernels, local(): pl.pallas_call(functools.partial(kernel, slabs, grps), out_shape=jax.Shap...  58.7 us
    unnamed x1, local copies, waits for them, and re-layouts  1.89 us

profile of v4, /device:TPU:1, one launch (start us, length us, event | category | flops | bytes accessed | tf_op | source)
XLA Modules:
  0.0 60.6 jit_solution(11738555650653173439)
XLA Ops:
  0.0 58.7 %shard_map.82 = f32[8,2,64,128]{3,2,1,0:T(8,128)} custom-call(f32[1,2,2,8]{3,2,1,0:T(2,128)} %dens_hbm.1, s32[1,2,2,8]{3,2,1,0:T(2,128)} %slots_hbm.1, s32[1,2,2,6]{3,2,1,0:T(2,128)} %neigh_hbm.1, s32[1,2,2,6]{3,2,1,0:T(2,128)} %codes_hbm.1, f32[64,64]{1,0:T(8,128)} %stiff_hbm.1, f32[8,64,64]{2,1,0:T(8,128)} %prolong_hbm.1, f32[16,64,64]{2,1,0:T(8,128)} %penalty_hbm.1, ...), custom_call_target="tpu_custom_call" | custom-call | tf_op jit(solution)/shard_map/pallas_call | solution.py:520
  58.7 1.9 %copy.11 = f32[8,2,2,4096]{3,2,1,0:T(2,128)} copy(f32[8,2,2,4096]{3,2,1,0:T(2,128)} %bitcast.10) | data formatting | bytes 1048576

commit v5 on v4

--- a/solution.py
+++ b/solution.py
@@ -65,9 +65,8 @@
     ops,
     pack,
     held,
-    weights,
-    rhs,
-    ijac,
+    base,
+    more,
     vec,
     part,
     g_up,
@@ -77,10 +76,13 @@
     total,
     top_1,
     top_2,
+    top_3,
     edge,
     edge_in,
     done,
     parts,
+    ready,
+    out_sems,
     rho_ss,
     rho_rs,
     held_ss,
@@ -89,6 +91,9 @@
     top1_rs,
     top2_ss,
     top2_rs,
+    top3_sems,
+    base_ss,
+    base_rs,
     edge_ss,
     edge_rs,
     parts_ss,
@@ -132,22 +137,35 @@
 
         lax.fori_loop(first, last, body, 0)
 
-    def device(step, d):
+    def device(d):
         chunk = lax.rem(mine + d, chunks)
-        return chunk, (chunk // 2, 2 * lax.rem(pair + step + pairs, pairs) + lax.rem(chunk, 2))
+        return chunk, (chunk // 2, 2 * pair + lax.rem(chunk, 2))
 
     def along(d):
         return (a, 2 * lax.rem(pair + d, pairs) + core)
 
+    near = pairs // 2
+
+    def around(d):
+        return (a, 2 * (pair // near * near + lax.rem(lax.rem(pair, near) + d, near)) + core)
+
+    opposite = along(near)
+    start, weights = base.at[:, 0:64], base.at[:, 64:88]
+    rhs, ijac = more.at[:, 0:64], more.at[:, 64:128]
+
     barrier = pltpu.get_barrier_semaphore()
 
     def greet(where):
         pl.semaphore_signal(barrier, inc=1, device_id=where, device_id_type=MESH)
 
-    steps = [0] + [sign * n for n in range(1, REACH + 1) for sign in (1, -1)]
-    for step in steps:
-        each(1 if step == 0 else 0, chunks, lambda d: greet(device(step, d)[1]))
-    each(REACH + 1, pairs - REACH, lambda d: greet(along(d)))
+    for d in range(1, chunks):
+        greet(device(d)[1])
+    greet(along(1))
+    greet(along(pairs - 1))
+    for d in range(1, near):
+        greet(around(d))
+    greet(opposite)
+    greet((a, lax.rem(b + grps - 1 + 2 * core, grps)))
 
     left = iota((64, 128), 1) < 64
 
@@ -158,27 +176,6 @@
             mean = mean + dens[0, l // 2, l % 2, c]
         rho[l : l + 1, :] = jnp.full((1, 128), mean * 0.125, f32)
     rho[4:8, :] = jnp.ones((4, 128), f32)
-
-    pl.semaphore_wait(barrier, (2 * REACH + 1) * chunks - 1 + max(0, pairs - 2 * REACH - 1))
-
-    def rho_copy(i, to_a, to_b):
-        return pltpu.make_async_remote_copy(
-            src_ref=rho,
-            dst_ref=rho_in.at[i],
-            send_sem=rho_ss.at[i],
-            recv_sem=rho_rs.at[i],
-            device_id=(to_a, to_b),
-            device_id_type=MESH,
-        )
-
-    rho_copies = [
-        rho_copy(DOWN_A, up_a, b),
-        rho_copy(UP_A, down_a, b),
-        rho_copy(DOWN_B, a, up_b),
-        rho_copy(UP_B, a, down_b),
-    ]
-    for copy in rho_copies:
-        copy.start()
 
     prolong_in.wait()
     for h in range(2):
@@ -237,6 +234,27 @@
         for i in range(2):
             ops[i, s * 32 : s * 32 + 32, 0:128] = two[i * 32 : i * 32 + 32]
             ops[i, s * 32 : s * 32 + 32, 128:192] = hi[i * 32 : i * 32 + 32]
+
+    pl.semaphore_wait(barrier, chunks - 1 + 2 + near - 1 + 1 + 1)
+
+    def rho_copy(i, to_a, to_b):
+        return pltpu.make_async_remote_copy(
+            src_ref=rho,
+            dst_ref=rho_in.at[i],
+            send_sem=rho_ss.at[i],
+            recv_sem=rho_rs.at[i],
+            device_id=(to_a, to_b),
+            device_id_type=MESH,
+        )
+
+    rho_copies = [
+        rho_copy(DOWN_A, up_a, b),
+        rho_copy(UP_A, down_a, b),
+        rho_copy(DOWN_B, a, up_b),
+        rho_copy(UP_B, a, down_b),
+    ]
+    for copy in rho_copies:
+        copy.start()
 
     neigh_in.wait()
     codes_in.wait()
@@ -274,20 +292,20 @@
     for chunk in range(chunks):
         pack[chunk, rows:, :] = tile
 
-    def held_copy(n, d):
-        chunk, where = device(steps[n], d)
+    def held_copy(d):
+        chunk, where = device(d)
         return pltpu.make_async_remote_copy(
             src_ref=pack.at[chunk],
-            dst_ref=held.at[2 * REACH - 2 * steps[n] + core, a],
-            send_sem=held_ss.at[n, d],
-            recv_sem=held_rs.at[n, d],
+            dst_ref=held.at[core, a],
+            send_sem=held_ss.at[d],
+            recv_sem=held_rs.at[d],
             device_id=where,
             device_id_type=MESH,
         )
 
-    for n in reversed(range(len(steps))):
-        each(1 if n == 0 else 0, chunks, lambda d: held_copy(n, d).start())
-    held[2 * REACH + core, a] = pack[mine]
+    for d in range(1, chunks):
+        held_copy(d).start()
+    held[core, a] = pack[mine]
 
     top = jnp.zeros((1, 1), f32)
     for m in range(2):
@@ -313,7 +331,7 @@
             dst_ref=top_1.at[d],
             send_sem=top1_ss.at[d],
             recv_sem=top1_rs.at[d],
-            device_id=device(0, d)[1],
+            device_id=device(d)[1],
             device_id_type=MESH,
         )
 
@@ -323,23 +341,21 @@
             dst_ref=top_2.at[d],
             send_sem=top2_ss.at[d],
             recv_sem=top2_rs.at[d],
-            device_id=along(d),
+            device_id=around(d),
             device_id_type=MESH,
         )
 
     each(1, chunks, lambda d: top1_copy(d).start())
 
-    for n in range(len(steps)):
-        each(1 if n == 0 else 0, chunks, lambda d: held_copy(n, d).wait())
     code16 = iota((16, 128), 0).astype(f32)
 
     def unpack(j, _):
-        got = held[j]
+        got = held[j - 2 * REACH]
         x = got[:, :rows, :].reshape(64, 128).T
         x = jnp.concatenate([x[:64], x[64:]], axis=1)
         meta = got[:, rows:, :].reshape(64, 128).T
         meta = jnp.concatenate([meta[0:32], meta[64:96]], axis=1)
-        weights[j] = meta
+        weights[j] = meta[0:24]
         summed = jnp.zeros((16, 128), f32)
         for face in range(6):
             summed = summed + jnp.where(
@@ -349,16 +365,11 @@
         over = 1.0 / mm(diags, table, highest)
         rhs[j] = x
         ijac[j] = over
+        start[j] = x * over
         vec[j] = x * over
         return 0
 
-    lax.fori_loop(0, UNITS, unpack, 0)
-
-    each(1, chunks, lambda d: top1_copy(d).wait())
-    top_2[0] = jnp.max(top_1[...], axis=0)
-    each(1, pairs, lambda d: top2_copy(d).start())
-
-    def products(t):
+    def products(t, which=None):
         def two(i, _):
             j = t // 2 + 2 * i
             hi, lo = split(jnp.concatenate([vec[j], vec[j + 1]], axis=1))
@@ -386,27 +397,70 @@
                     g_down[j + u, at, :] = g[DOWN_B]
             return 0
 
-        lax.fori_loop(0, UNITS // 2 - t // 2, two, 0)
+        if which is None:
+            lax.fori_loop(0, UNITS // 2 - t // 2, two, 0)
+        else:
+            lax.fori_loop(0, len(which), lambda i, _: two(which[0] + (which[-1] - which[0]) * i, 0), 0)
 
     def applied(t, use):
         def one(j, _):
-            below, above = jnp.maximum(j - 1, 0), jnp.minimum(j + 1, UNITS - 1)
+            below, above = max(j - 1, 0), min(j + 1, UNITS - 1)
             low = roll(jnp.where(left, g_up[j], g_up[below]), 64)
             high = roll(jnp.where(left, g_down[above], g_down[j]), 64)
             use(j, part[j] - low - high)
             return 0
 
-        lax.fori_loop((t + 1) // 2, UNITS - (t + 1) // 2, one, 0)
+        for j in range((t + 1) // 2, UNITS - (t + 1) // 2):
+            one(j, 0)
 
     def keep_first(j, value):
         w0[j] = value
         vec[j] = value * ijac[j]
 
-    products(0)
+    each(1, chunks, lambda d: held_copy(d).wait())
+    for j in range(2 * REACH, 2 * REACH + 2):
+        unpack(j, 0)
+
+    def base_copy(n, ref, side, d):
+        return pltpu.make_async_remote_copy(
+            src_ref=ref.at[2:4],
+            dst_ref=ref.at[4 * side : 4 * side + 2],
+            send_sem=base_ss.at[n, side],
+            recv_sem=base_rs.at[n, side],
+            device_id=along(d),
+            device_id_type=MESH,
+        )
+
+    base_copies = [base_copy(0, base, 0, 1), base_copy(0, base, 1, pairs - 1)]
+    more_copies = [base_copy(1, more, 0, 1), base_copy(1, more, 1, pairs - 1)]
+    for copy in base_copies + more_copies:
+        copy.start()
+    products(0, (REACH,))
+    each(1, chunks, lambda d: top1_copy(d).wait())
+    top_2[0] = jnp.max(top_1[...], axis=0)
+    each(1, near, lambda d: top2_copy(d).start())
+    for copy in base_copies:
+        copy.wait()
+    for j in (0, 1, 4, 5):
+        vec[j] = start[j]
+    products(0, (0, 2 * REACH))
+    for copy in more_copies:
+        copy.wait()
     applied(0, keep_first)
+    each(1, near, lambda d: top2_copy(d).wait())
+    top_3[0] = jnp.max(top_2[...], axis=0)
+    top3_copy = pltpu.make_async_remote_copy(
+        src_ref=top_3.at[0],
+        dst_ref=top_3.at[1],
+        send_sem=top3_sems.at[0],
+        recv_sem=top3_sems.at[1],
+        device_id=opposite,
+        device_id_type=MESH,
+    )
+    top3_copy.start()
     products(1)
-    each(1, pairs, lambda d: top2_copy(d).wait())
-    upper = jnp.max(top_2[...], axis=0)[0:1, :]
+    top3_copy.wait()
+    upper = jnp.max(top_3[...], axis=0)[0:1, :]
 
     lower = upper / 10.0
     centre_val = 0.5 * (upper + lower)
@@ -433,7 +487,7 @@
 
     applied(1, combine)
 
-    def sweep(t, damp):
+    def sweep(t, damp, multiply=products):
         damp_next = 1.0 / (2.0 * sigma - damp)
         keep, gain = damp_next * damp, 2.0 * damp_next / half_width
 
@@ -444,41 +498,55 @@
             total[j] = total[j] + update
             vec[j] = update
 
-        products(t)
+        multiply(t)
         applied(t, step)
         return damp_next
 
-    damp = lax.fori_loop(2, SPAN, sweep, damp2)
+    damp = damp2
+    for t in range(2, SPAN):
+        damp = sweep(t, damp)
 
     edge[0] = vec[2 * REACH : 2 * REACH + 2]
     edge[1] = resid[2 * REACH : 2 * REACH + 2]
 
-    def edge_copy(side, d):
+    def edge_copy(n, side, d):
         return pltpu.make_async_remote_copy(
-            src_ref=edge,
-            dst_ref=edge_in.at[side],
-            send_sem=edge_ss.at[side],
-            recv_sem=edge_rs.at[side],
+            src_ref=edge.at[n],
+            dst_ref=edge_in.at[side, n],
+            send_sem=edge_ss.at[n, side],
+            recv_sem=edge_rs.at[n, side],
             device_id=along(d),
             device_id_type=MESH,
         )
 
-    edge_copies = [edge_copy(0, 1), edge_copy(1, pairs - 1)]
-    for copy in edge_copies:
+    vec_copies, resid_copies = [
+        [edge_copy(n, 0, 1), edge_copy(n, 1, pairs - 1)] for n in range(2)
+    ]
+    for copy in vec_copies + resid_copies:
         copy.start()
-    for copy in edge_copies:
+    products(0, (REACH,))
+    for copy in vec_copies:
         copy.wait()
     for side in range(2):
         vec[4 * side : 4 * side + 2] = edge_in[side, 0]
-        resid[4 * side : 4 * side + 2] = edge_in[side, 1]
-    lax.fori_loop(0, SWEEPS - SPAN, sweep, damp)
+
+    def outer(t):
+        products(t, (0, 2 * REACH))
+        for copy in resid_copies:
+            copy.wait()
+        for side in range(2):
+            resid[4 * side : 4 * side + 2] = edge_in[side, 1]
+
+    damp = sweep(0, damp, outer)
+    for t in range(1, SWEEPS - SPAN):
+        damp = sweep(t, damp)
 
     for u in range(2):
         x = total[2 * REACH + u]
         done[u] = jnp.concatenate([x[:, :64], x[:, 64:]], axis=0).T
 
     def parts_copy(d):
-        chunk, where = device(0, d)
+        chunk, where = device(d)
         return pltpu.make_async_remote_copy(
             src_ref=done.at[lax.rem(chunk, 2)],
             dst_ref=parts.at[mine],
@@ -494,18 +562,24 @@
 
     even = lax.rem(iota((64, 128), 0), 2) == 0
 
+    def out_copy(i):
+        return pltpu.make_async_copy(ready.at[i], out.at[i], out_sems.at[i])
+
     def place(i, _):
-        at = pl.ds(pl.multiple_of(i * rows, rows), rows)
+        at = pl.ds(i * rows, rows)
         hi, lo = split(parts[:, at, :].reshape(128, 128).T)
         x = mm(hi, order) + mm(lo, order)
         for m in range(2):
             own = x[m * 64 : m * 64 + 64]
             turned = roll(own, 64)
             moved = jnp.where(even, pltpu.roll(turned, 63, 0), pltpu.roll(turned, 1, 0))
-            out[i, m] = jnp.where(even == left, own, moved)
+            ready[i, m] = jnp.where(even == left, own, moved)
+        out_copy(i).start()
         return 0
 
-    lax.fori_loop(0, slabs, place, 0)
+    for i in range(slabs):
+        place(i, 0)
+    each(0, slabs, lambda i: out_copy(i).wait())
 
 
 def local(slabs, grps, dens, slots, neigh, codes, stiff, prolong, penalty, fine):
@@ -515,13 +589,12 @@
     dma = pltpu.SemaphoreType.DMA
     chunks, pairs = 2 * slabs, grps // 2
     rows = 128 // chunks
-    reach = 2 * REACH + 1
     columns = pltpu.VMEM((UNITS, 64, 128), f32)
     result = pl.pallas_call(
         functools.partial(kernel, slabs, grps),
         out_shape=jax.ShapeDtypeStruct((slabs, 2, 64, 128), f32),
         in_specs=[pl.BlockSpec(memory_space=pl.ANY)] * 8,
-        out_specs=pl.BlockSpec(memory_space=pltpu.VMEM),
+        out_specs=pl.BlockSpec(memory_space=pl.ANY),
         scratch_shapes=[
             *(space(v.shape, v.dtype) for space, v in zip([smem] * 4 + [vmem] * 4, args)),
             dma((8,)),
@@ -531,25 +604,32 @@
             pltpu.VMEM((256, 128), f32),
             pltpu.VMEM((2, 768, 192), bf16),
             pltpu.VMEM((chunks, 2 * rows, 128), f32),
-            pltpu.VMEM((UNITS, slabs, 2 * rows, 128), f32),
-            pltpu.VMEM((UNITS, 32, 128), f32),
-            *[columns] * 9,
+            pltpu.VMEM((2, slabs, 2 * rows, 128), f32),
+            pltpu.VMEM((UNITS, 88, 128), f32),
+            pltpu.VMEM((UNITS, 128, 128), f32),
+            *[columns] * 7,
             pltpu.VMEM((chunks, 8, 128), f32),
-            pltpu.VMEM((pairs, 8, 128), f32),
+            pltpu.VMEM((pairs // 2, 8, 128), f32),
+            pltpu.VMEM((2, 8, 128), f32),
             pltpu.VMEM((2, 2, 64, 128), f32),
             pltpu.VMEM((2, 2, 2, 64, 128), f32),
             pltpu.VMEM((2, 64, 128), f32),
             pltpu.VMEM((chunks, 64, 128), f32),
+            pltpu.VMEM((slabs, 2, 64, 128), f32),
+            dma((slabs,)),
             dma((4,)),
             dma((4,)),
-            dma((reach, chunks)),
-            dma((reach, chunks)),
             dma((chunks,)),
             dma((chunks,)),
-            dma((pairs,)),
-            dma((pairs,)),
+            dma((chunks,)),
+            dma((chunks,)),
+            dma((pairs // 2,)),
+            dma((pairs // 2,)),
             dma((2,)),
-            dma((2,)),
+            dma((2, 2)),
+            dma((2, 2)),
+            dma((2, 2)),
+            dma((2, 2)),
             dma((chunks,)),
             dma((chunks,)),
         ],

time: 60.7 us -> 54.8 us (0.903)
  Pallas kernels: 58.7 us -> 52.7 us
    pallas_call x1, Pallas kernels: 58.7 us -> 52.7 us  [local(): pl.pallas_call(functools.partial(kernel, slabs, grps), out_shape=jax.Shap...]
where the time goes in v5:
time: 54.8 us; the launch traced here: 54.6 us
  Pallas kernels  52.7 us (96%)
  local copies, waits for them, and re-layouts  1.89 us (3%)
    pallas_call x1, Pallas kernels, local(): pl.pallas_call(functools.partial(kernel, slabs, grps), out_shape=jax.Shap...  52.7 us
    unnamed x1, local copies, waits for them, and re-layouts  1.89 us

profile of v5, /device:TPU:1, one launch (start us, length us, event | category | flops | bytes accessed | tf_op | source)
XLA Modules:
  0.0 54.6 jit_solution(15275848842545414051)
XLA Ops:
  0.0 52.7 %shard_map.82 = f32[8,2,64,128]{3,2,1,0:T(8,128)} custom-call(f32[1,2,2,8]{3,2,1,0:T(2,128)} %dens_hbm.1, s32[1,2,2,8]{3,2,1,0:T(2,128)} %slots_hbm.1, s32[1,2,2,6]{3,2,1,0:T(2,128)} %neigh_hbm.1, s32[1,2,2,6]{3,2,1,0:T(2,128)} %codes_hbm.1, f32[64,64]{1,0:T(8,128)} %stiff_hbm.1, f32[8,64,64]{2,1,0:T(8,128)} %prolong_hbm.1, f32[16,64,64]{2,1,0:T(8,128)} %penalty_hbm.1, ...), custom_call_target="tpu_custom_call" | custom-call | tf_op jit(solution)/shard_map/pallas_call | solution.py:593
  52.7 1.9 %copy.11 = f32[8,2,2,4096]{3,2,1,0:T(2,128)} copy(f32[8,2,2,4096]{3,2,1,0:T(2,128)} %bitcast.10) | data formatting | bytes 1048576

commit v6 on v5

--- a/solution.py
+++ b/solution.py
@@ -369,6 +369,8 @@
         vec[j] = x * over
         return 0
 
+    own_units = range(2 * REACH, 2 * REACH + 2)
+
     def products(t, which=None):
         def two(i, _):
             j = t // 2 + 2 * i
@@ -380,16 +382,26 @@
                 for u in range(2):
                     y = every[:, u * 128 : u * 128 + 128]
                     w = weights.at[j + u]
+
+                    def flux_of(face):
+                        code = jnp.broadcast_to(w[8 + face : 9 + face, :], (32, 128))
+                        flux = y[256:288]
+                        for c in range(1, 16):
+                            flux = jnp.where(code == c, y[256 + c * 32 : 288 + c * 32], flux)
+                        return w[14 + face : 15 + face, :] * flux
+
+                    if j + u < (t + 1) // 2:
+                        g_up[j + u, at, :] = flux_of(UP_B)
+                        continue
+                    if j + u >= UNITS - (t + 1) // 2:
+                        g_down[j + u, at, :] = flux_of(DOWN_B)
+                        continue
                     result = w[0:1, :] * y[0:32]
                     for s in range(1, 8):
                         result = result + w[s : s + 1, :] * y[s * 32 : s * 32 + 32]
                     g = []
                     for face in range(6):
-                        code = jnp.broadcast_to(w[8 + face : 9 + face, :], (32, 128))
-                        flux = y[256:288]
-                        for c in range(1, 16):
-                            flux = jnp.where(code == c, y[256 + c * 32 : 288 + c * 32], flux)
-                        g.append(w[14 + face : 15 + face, :] * flux)
+                        g.append(flux_of(face))
                         result = result + g[face]
                     result = result - roll(g[UP_A], rows) - roll(g[DOWN_A], -rows)
                     part[j + u, at, :] = result - roll(g[UP_C], q) - roll(g[DOWN_C], -q)
@@ -397,10 +409,8 @@
                     g_down[j + u, at, :] = g[DOWN_B]
             return 0
 
-        if which is None:
-            lax.fori_loop(0, UNITS // 2 - t // 2, two, 0)
-        else:
-            lax.fori_loop(0, len(which), lambda i, _: two(which[0] + (which[-1] - which[0]) * i, 0), 0)
+        for i in range(UNITS // 2 - t // 2) if which is None else which:
+            two(i, 0)
 
     def applied(t, use):
         def one(j, _):
@@ -482,7 +492,8 @@
         resid2 = resid1 - both
         update2 = keep2 * update1 + gain2 * (resid2 * over)
         resid[j] = resid2
-        total[j] = update0 + update1 + update2
+        if j in own_units:
+            total[j - 2 * REACH] = update0 + update1 + update2
         vec[j] = update2
 
     applied(1, combine)
@@ -495,7 +506,8 @@
             now = resid[j] - value
             resid[j] = now
             update = keep * vec[j] + gain * (now * ijac[j])
-            total[j] = total[j] + update
+            if j in own_units:
+                total[j - 2 * REACH] = total[j - 2 * REACH] + update
             vec[j] = update
 
         multiply(t)
@@ -542,7 +554,7 @@
         damp = sweep(t, damp)
 
     for u in range(2):
-        x = total[2 * REACH + u]
+        x = total[u]
         done[u] = jnp.concatenate([x[:, :64], x[:, 64:]], axis=0).T
 
     def parts_copy(d):
@@ -607,7 +619,8 @@
             pltpu.VMEM((2, slabs, 2 * rows, 128), f32),
             pltpu.VMEM((UNITS, 88, 128), f32),
             pltpu.VMEM((UNITS, 128, 128), f32),
-            *[columns] * 7,
+            *[columns] * 6,
+            pltpu.VMEM((2, 64, 128), f32),
             pltpu.VMEM((chunks, 8, 128), f32),
             pltpu.VMEM((pairs // 2, 8, 128), f32),
             pltpu.VMEM((2, 8, 128), f32),

time: 54.8 us -> 51.4 us (0.938)
  Pallas kernels: 52.7 us -> 49.3 us
    pallas_call x1, Pallas kernels: 52.7 us -> 49.3 us  [local(): pl.pallas_call(functools.partial(kernel, slabs, grps), out_shape=jax.Shap...]
where the time goes in v6:
time: 51.4 us; the launch traced here: 51.2 us
  Pallas kernels  49.3 us (96%)
  local copies, waits for them, and re-layouts  1.89 us (4%)
    pallas_call x1, Pallas kernels, local(): pl.pallas_call(functools.partial(kernel, slabs, grps), out_shape=jax.Shap...  49.3 us
    unnamed x1, local copies, waits for them, and re-layouts  1.89 us

profile of v6, /device:TPU:1, one launch (start us, length us, event | category | flops | bytes accessed | tf_op | source)
XLA Modules:
  0.0 51.2 jit_solution(9154539427324168719)
XLA Ops:
  0.0 49.3 %shard_map.82 = f32[8,2,64,128]{3,2,1,0:T(8,128)} custom-call(f32[1,2,2,8]{3,2,1,0:T(2,128)} %dens_hbm.1, s32[1,2,2,8]{3,2,1,0:T(2,128)} %slots_hbm.1, s32[1,2,2,6]{3,2,1,0:T(2,128)} %neigh_hbm.1, s32[1,2,2,6]{3,2,1,0:T(2,128)} %codes_hbm.1, f32[64,64]{1,0:T(8,128)} %stiff_hbm.1, f32[8,64,64]{2,1,0:T(8,128)} %prolong_hbm.1, f32[16,64,64]{2,1,0:T(8,128)} %penalty_hbm.1, ...), custom_call_target="tpu_custom_call" | custom-call | tf_op jit(solution)/shard_map/pallas_call | solution.py:605
  49.4 1.9 %copy.11 = f32[8,2,2,4096]{3,2,1,0:T(2,128)} copy(f32[8,2,2,4096]{3,2,1,0:T(2,128)} %bitcast.10) | data formatting | bytes 1048576

commit v7 on v6

--- a/solution.py
+++ b/solution.py
@@ -137,6 +137,12 @@
 
         lax.fori_loop(first, last, body, 0)
 
+    ring = slabs // 2
+    far_first = sorted(
+        range(1, chunks),
+        key=lambda d: -min(d // 2 % ring, ring - d // 2 % ring) - (d // 2 >= ring),
+    )
+
     def device(d):
         chunk = lax.rem(mine + d, chunks)
         return chunk, (chunk // 2, 2 * pair + lax.rem(chunk, 2))
@@ -303,7 +309,7 @@
             device_id_type=MESH,
         )
 
-    for d in range(1, chunks):
+    for d in far_first:
         held_copy(d).start()
     held[core, a] = pack[mine]
 
@@ -568,7 +574,8 @@
             device_id_type=MESH,
         )
 
-    each(1, chunks, lambda d: parts_copy(d).start())
+    for d in far_first:
+        parts_copy(d).start()
     parts[mine] = done[core]
     each(1, chunks, lambda d: parts_copy(d).wait())
 

time: 51.4 us -> 51 us (level)
  no operation moved by 1% of the time
where the time goes in v7:
time: 51 us; the launch traced here: 50.8 us
  Pallas kernels  48.9 us (96%)
  local copies, waits for them, and re-layouts  1.89 us (4%)
    pallas_call x1, Pallas kernels, local(): pl.pallas_call(functools.partial(kernel, slabs, grps), out_shape=jax.Shap...  48.9 us
    unnamed x1, local copies, waits for them, and re-layouts  1.89 us

profile of v7, /device:TPU:1, one launch (start us, length us, event | category | flops | bytes accessed | tf_op | source)
XLA Modules:
  0.0 50.8 jit_solution(16072549415821414369)
XLA Ops:
  0.0 48.9 %shard_map.82 = f32[8,2,64,128]{3,2,1,0:T(8,128)} custom-call(f32[1,2,2,8]{3,2,1,0:T(2,128)} %dens_hbm.1, s32[1,2,2,8]{3,2,1,0:T(2,128)} %slots_hbm.1, s32[1,2,2,6]{3,2,1,0:T(2,128)} %neigh_hbm.1, s32[1,2,2,6]{3,2,1,0:T(2,128)} %codes_hbm.1, f32[64,64]{1,0:T(8,128)} %stiff_hbm.1, f32[8,64,64]{2,1,0:T(8,128)} %prolong_hbm.1, f32[16,64,64]{2,1,0:T(8,128)} %penalty_hbm.1, ...), custom_call_target="tpu_custom_call" | custom-call | tf_op jit(solution)/shard_map/pallas_call | solution.py:612
  48.9 1.9 %copy.11 = f32[8,2,2,4096]{3,2,1,0:T(2,128)} copy(f32[8,2,2,4096]{3,2,1,0:T(2,128)} %bitcast.10) | data formatting | bytes 1048576
